TPU v7x, 32 devices: a whole 2x2x4 slice. The times are simulated.
32 devices in a mesh: dp: 4 (over z), seq: 4 (over y, x), mp: 2 (over core).
Axes of the slice: x: 2, y: 2, z: 4, core: 2. Of those that a mesh axis runs over, the one named last changes fastest.
Arguments:
- inputs: bfloat16 [8, 4096, 768], P('dp', 'seq'), may hold values from -8 to 8
- cotangent: bfloat16 [8, 4096, 768], P('dp', 'seq'), may hold values from -8 to 8
- padding: int32 [8, 4096], P('dp'), may hold values from 0 to 1, as said below
- documents: int32 [8, 4096], P('dp'), may hold values from 0 to 8, as said below
- w_query: bfloat16 [768, 768], P(None, 'mp'), may hold values from -0.75 to 0.75
- w_key: bfloat16 [768, 768], P(None, 'mp'), may hold values from -0.75 to 0.75
- w_value: bfloat16 [768, 768], P(None, 'mp'), may hold values from -0.4375 to 0.4375
- w_out: bfloat16 [768, 768], P('mp'), may hold values from -0.21875 to 0.21875
- w_up: bfloat16 [768, 3072], P(None, 'mp'), may hold values from -0.21875 to 0.21875
- w_down: bfloat16 [3072, 768], P('mp'), may hold values from -0.109375 to 0.109375
- conv_taps: float32 [12, 33], P('mp'), may hold values from -2.5 to 2.5
- gain_attn: float32 [768], replicated, may hold values from 0.5 to 1.5
- shift_attn: float32 [768], replicated, may hold values from -1.25 to 1.25
- gain_ffn: float32 [768], replicated, may hold values from 0.5 to 1.5
- shift_ffn: float32 [768], replicated, may hold values from -1.25 to 1.25
Outputs:
- outputs: bfloat16 [8, 4096, 768], P('dp', 'seq')
- grad_inputs: bfloat16 [8, 4096, 768], P('dp', 'seq', 'mp')
- grad_query: float32 [768, 768], P(('dp', 'seq'), 'mp')
- grad_key: float32 [768, 768], P(('dp', 'seq'), 'mp')
- grad_value: float32 [768, 768], P(('dp', 'seq'), 'mp')
- grad_out: float32 [768, 768], P('mp', ('dp', 'seq'))
- grad_up: float32 [768, 3072], P(('dp', 'seq'), 'mp')
- grad_down: float32 [3072, 768], P('mp', ('dp', 'seq'))
- grad_taps: float32 [12, 33], P('mp')
- grad_gain_attn: float32 [768], replicated
- grad_shift_attn: float32 [768], replicated
- grad_gain_ffn: float32 [768], replicated
- grad_shift_ffn: float32 [768], replicated
- row_rms: float32 [8, 3], P('dp')
Inputs may be any that keep to these rules, and one draw needn't show every extreme that they name: `padding`: each row is 1 on a leading run of at least 3072 positions and 0 after it. `documents`: never falls along a row; position 0 of every row is in document 0; positions 512 to 3583 of a row lie in one document.
All inputs are finite; a program needn't handle non-finite values.
Results may differ from a plain program's by a relative error of at most 0.035.
Values may be sent and summed in bfloat16 or wider, within the bound.
A program may use at most 192 MiB of HBM per device.

v0:
```python
import math

import jax
import jax.numpy as jnp
from jax import lax
from jax.sharding import PartitionSpec as P

M = 64
ITERS = 6
LEN = 4096


highest = lax.Precision.HIGHEST


def with_halo(array, sides, width):
    for axis, dim in sides:
        count, length = (lax.axis_size(axis), array.shape[dim])
        up = [(i, (i + 1) % count) for i in range(count - 1)]
        down = [(j, i) for i, j in up]
        last = lax.slice_in_dim(array, length - width, length, axis=dim)
        leading = lax.slice_in_dim(array, 0, width, axis=dim)
        before = lax.ppermute(last, axis, up)
        after = lax.ppermute(leading, axis, down)
        array = jnp.concatenate([before, array, after], axis=dim)
    return array


def pseudo_inverse(kernel):
    size = kernel.shape[-1]
    ident = jnp.eye(size, dtype=kernel.dtype)
    scale = 1.0 / jnp.max(jnp.sum(kernel, axis=-2), axis=-1)
    approx = jnp.swapaxes(kernel, -1, -2) * scale[..., None, None]
    for section in range(ITERS):
        product = jnp.matmul(kernel, approx, precision=highest)
        inner = 7.0 * ident - product
        inner = 15.0 * ident - jnp.matmul(product, inner, precision=highest)
        inner = 13.0 * ident - jnp.matmul(product, inner, precision=highest)
        approx = 0.25 * jnp.matmul(approx, inner, precision=highest)
    return approx


def norm_layer(hidden, gain, shift):
    centre = hidden - jnp.mean(hidden, axis=-1, keepdims=True)
    spread = jnp.mean(centre * centre, axis=-1, keepdims=True)
    return centre * lax.rsqrt(spread + 1e-05) * gain + shift


def gelu_exact(values):
    return jax.nn.gelu(values, approximate=False)


def left_product(left, right):
    return lax.dot_general(
        left, right, (((0,), (0,)), ((), ())), preferred_element_type=jnp.float32
    )


def right_product(left, right):
    return lax.dot_general(
        left, right, (((1,), (1,)), ((), ())), preferred_element_type=jnp.float32
    )


def shards(
    inputs,
    cotangent,
    padding,
    documents,
    w_query,
    w_key,
    w_value,
    w_out,
    w_up,
    w_down,
    conv_taps,
    gain_attn,
    shift_attn,
    gain_ffn,
    shift_ffn,
):
    row_count, tok_count, model_width = inputs.shape
    local_width = w_query.shape[1]
    head_count, tap_count = conv_taps.shape
    head_dim = local_width // head_count
    half_taps = tap_count // 2
    seg_len = LEN // M
    local_marks = tok_count // seg_len
    flat_rows = row_count * tok_count
    seq_place = lax.axis_index("seq")
    keep_full = padding.astype(jnp.float32)
    row_valid = jnp.sum(keep_full, axis=1)
    keep = lax.dynamic_slice_in_dim(keep_full, seq_place * tok_count, tok_count, 1)
    keep_flat = keep.reshape(flat_rows, 1)
    x_flat = inputs.reshape(flat_rows, model_width)
    input_float = x_flat.astype(jnp.float32)
    queries = jnp.dot(x_flat, w_query, preferred_element_type=jnp.float32).astype(jnp.bfloat16)
    key_rows = jnp.dot(x_flat, w_key, preferred_element_type=jnp.float32).astype(jnp.bfloat16)
    value_rows = jnp.dot(x_flat, w_value, preferred_element_type=jnp.float32).astype(
        jnp.bfloat16
    ) * keep_flat.astype(jnp.bfloat16)
    counts = jnp.sum(keep.reshape(row_count, local_marks, seg_len), axis=2)
    denom = jnp.maximum(counts, 1.0)[..., None]

    def landmark(rows):
        summed = jnp.sum(
            (rows.astype(jnp.float32) * keep_flat).reshape(
                row_count, local_marks, seg_len, local_width
            ),
            axis=2,
        )
        return (summed / denom).astype(jnp.bfloat16)

    query_marks, key_marks = (
        lax.all_gather(landmark(queries), "seq", axis=1, tiled=True),
        lax.all_gather(landmark(key_rows), "seq", axis=1, tiled=True),
    )
    q_heads = queries.reshape(row_count, tok_count, head_count, head_dim)
    k_heads = key_rows.reshape(row_count, tok_count, head_count, head_dim)
    v_heads = value_rows.reshape(row_count, tok_count, head_count, head_dim)
    q_marks = query_marks.reshape(row_count, M, head_count, head_dim)
    k_marks = key_marks.reshape(row_count, M, head_count, head_dim)
    score_one = (
        jnp.einsum("rthe,rmhe->rthm", q_heads, k_marks, preferred_element_type=jnp.float32) * 0.125
    )
    kernel_one = jax.nn.softmax(score_one, axis=-1)
    kernel_low = kernel_one.astype(jnp.bfloat16)
    score_two = (
        jnp.einsum("rahe,rbhe->rhab", q_marks, k_marks, preferred_element_type=jnp.float32) * 0.125
    )
    kernel_two = jax.nn.softmax(score_two, axis=-1)
    inverse, inverse_back = jax.vjp(pseudo_inverse, kernel_two)
    score_three = (
        jnp.einsum("rmhe,rthe->rhmt", q_marks, k_heads, preferred_element_type=jnp.float32) * 0.125
    )
    masked = score_three - (1.0 - keep)[:, None, None, :] * 1000000000.0
    top = lax.pmax(jnp.max(masked, axis=-1), "seq")
    exp_local = jnp.exp(masked - top[..., None])
    mixed_local = jnp.einsum(
        "rhmt,rthe->rhme",
        exp_local.astype(jnp.bfloat16),
        v_heads,
        preferred_element_type=jnp.float32,
    )
    totals, mixed = lax.psum((jnp.sum(exp_local, axis=-1), mixed_local), "seq")
    landmark_values = mixed / totals[..., None]
    context_mix = jnp.einsum("rhab,rhbe->rhae", inverse, landmark_values, precision=highest).astype(
        jnp.bfloat16
    )
    attended = jnp.einsum(
        "rthm,rhme->rthe", kernel_low, context_mix, preferred_element_type=jnp.float32
    ).reshape(row_count, tok_count, local_width)
    value_rims = with_halo(
        value_rows.reshape(row_count, tok_count, local_width), (("seq", 1),), half_taps
    )
    padded_docs = jnp.pad(documents, ((0, 0), (half_taps, half_taps)), constant_values=-1)
    doc_window = lax.dynamic_slice_in_dim(
        padded_docs, seq_place * tok_count, tok_count + 2 * half_taps, 1
    )
    own_docs = doc_window[:, half_taps : half_taps + tok_count]
    tap_weights = jnp.repeat(conv_taps, head_dim, axis=0)
    conv_sum = jnp.zeros((row_count, tok_count, local_width), jnp.float32)
    for offset in range(tap_count):
        same_doc = (doc_window[:, offset : offset + tok_count] == own_docs).astype(jnp.float32)[
            ..., None
        ]
        conv_sum = (
            conv_sum
            + tap_weights[:, offset]
            * value_rims[:, offset : offset + tok_count].astype(jnp.float32)
            * same_doc
        )
    context = (attended + conv_sum).astype(jnp.bfloat16).reshape(flat_rows, local_width)
    branch_attn = lax.psum(jnp.dot(context, w_out, preferred_element_type=jnp.float32), "mp")
    normed, norm_attn_back = jax.vjp(norm_layer, input_float + branch_attn, gain_attn, shift_attn)
    normed_low = normed.astype(jnp.bfloat16)
    up_rows = jnp.dot(normed_low, w_up, preferred_element_type=jnp.float32)
    activated, gelu_back = jax.vjp(gelu_exact, up_rows)
    act_low = activated.astype(jnp.bfloat16)
    branch_ffn = lax.psum(jnp.dot(act_low, w_down, preferred_element_type=jnp.float32), "mp")
    result, norm_ffn_back = jax.vjp(norm_layer, normed + branch_ffn, gain_ffn, shift_ffn)
    outputs = result.astype(jnp.bfloat16).reshape(row_count, tok_count, model_width)

    def row_squares(values):
        return jnp.sum(
            (jnp.sum(values * values, axis=1) * keep.reshape(flat_rows)).reshape(
                row_count, tok_count
            ),
            axis=1,
        )

    square_terms = jnp.stack(
        [row_squares(input_float), row_squares(branch_attn), row_squares(branch_ffn)], axis=1
    )
    grad_result = cotangent.reshape(flat_rows, model_width).astype(jnp.float32)
    grad_h2, grad_gain_ffn, grad_shift_ffn = norm_ffn_back(grad_result)
    grad_branch = grad_h2.astype(jnp.bfloat16)
    grad_down = left_product(act_low, grad_branch)
    grad_act = right_product(grad_branch, w_down)
    grad_up_rows = gelu_back(grad_act)[0].astype(jnp.bfloat16)
    grad_up = left_product(normed_low, grad_up_rows)
    grad_normed = grad_h2 + lax.psum(right_product(grad_up_rows, w_up), "mp")
    grad_h1, grad_gain_attn, grad_shift_attn = norm_attn_back(grad_normed)
    grad_attn = grad_h1.astype(jnp.bfloat16)
    grad_out_w = left_product(context, grad_attn)
    grad_context = right_product(grad_attn, w_out).astype(jnp.bfloat16)
    grad_ctx_heads = grad_context.reshape(row_count, tok_count, head_count, head_dim)
    grad_kernel_one = jnp.einsum(
        "rthe,rhme->rthm", grad_ctx_heads, context_mix, preferred_element_type=jnp.float32
    )
    grad_mix_local = jnp.einsum(
        "rthm,rthe->rhme", kernel_low, grad_ctx_heads, preferred_element_type=jnp.float32
    )
    grad_mix, square_sums = lax.psum((grad_mix_local, square_terms), "seq")
    grad_inverse = jnp.einsum("rhae,rhbe->rhab", grad_mix, landmark_values, precision=highest)
    grad_landmark_values = jnp.einsum("rhab,rhae->rhbe", inverse, grad_mix, precision=highest)
    exp_global = jnp.exp(masked - top[..., None])
    grad_mixed = (grad_landmark_values / totals[..., None]).astype(jnp.bfloat16)
    grad_totals = -jnp.sum(grad_landmark_values * landmark_values, axis=-1) / totals
    grad_exp = (
        jnp.einsum("rhme,rthe->rhmt", grad_mixed, v_heads, preferred_element_type=jnp.float32)
        + grad_totals[..., None]
    )
    grad_three = (exp_global * grad_exp).astype(jnp.bfloat16)
    grad_query_three = (
        jnp.einsum("rhmt,rthe->rmhe", grad_three, k_heads, preferred_element_type=jnp.float32)
        * 0.125
    )
    grad_key_three = (
        jnp.einsum("rhmt,rmhe->rthe", grad_three, q_marks, preferred_element_type=jnp.float32)
        * 0.125
    )
    grad_value_three = jnp.einsum(
        "rhmt,rhme->rthe",
        exp_global.astype(jnp.bfloat16),
        grad_mixed,
        preferred_element_type=jnp.float32,
    )
    inner_one = jnp.sum(grad_kernel_one * kernel_one, axis=-1, keepdims=True)
    grad_one = (kernel_one * (grad_kernel_one - inner_one)).astype(jnp.bfloat16)
    grad_query_one = (
        jnp.einsum("rthm,rmhe->rthe", grad_one, k_marks, preferred_element_type=jnp.float32) * 0.125
    )
    grad_keymark_one = (
        jnp.einsum("rthm,rthe->rmhe", grad_one, q_heads, preferred_element_type=jnp.float32) * 0.125
    )
    grad_kernel_two = inverse_back(grad_inverse)[0]
    inner_two = jnp.sum(grad_kernel_two * kernel_two, axis=-1, keepdims=True)
    grad_two = kernel_two * (grad_kernel_two - inner_two)
    grad_query_two = (
        jnp.einsum("rhab,rbhe->rahe", grad_two, k_marks.astype(jnp.float32), precision=highest)
        * 0.125
    )
    grad_keymark_two = (
        jnp.einsum("rhab,rahe->rbhe", grad_two, q_marks.astype(jnp.float32), precision=highest)
        * 0.125
    )
    grad_qmark_local, grad_kmark_local = (
        lax.psum_scatter(
            grad_query_three.reshape(row_count, M, local_width),
            "seq",
            scatter_dimension=1,
            tiled=True,
        ),
        lax.psum_scatter(
            grad_keymark_one.reshape(row_count, M, local_width),
            "seq",
            scatter_dimension=1,
            tiled=True,
        ),
    )
    mark_start = seq_place * local_marks
    grad_qmark = grad_qmark_local + lax.dynamic_slice_in_dim(
        grad_query_two.reshape(row_count, M, local_width), mark_start, local_marks, 1
    )
    grad_kmark = grad_kmark_local + lax.dynamic_slice_in_dim(
        grad_keymark_two.reshape(row_count, M, local_width), mark_start, local_marks, 1
    )

    def spread_marks(grad_mark):
        shared = jnp.broadcast_to(
            (grad_mark / denom)[:, :, None, :], (row_count, local_marks, seg_len, local_width)
        )
        return shared.reshape(flat_rows, local_width) * keep_flat

    grad_queries = (
        grad_query_one.reshape(flat_rows, local_width) + spread_marks(grad_qmark)
    ).astype(jnp.bfloat16)
    grad_keys = (grad_key_three.reshape(flat_rows, local_width) + spread_marks(grad_kmark)).astype(
        jnp.bfloat16
    )
    grad_rims = with_halo(
        grad_context.reshape(row_count, tok_count, local_width), (("seq", 1),), half_taps
    )
    grad_conv_value = jnp.zeros((row_count, tok_count, local_width), jnp.float32)
    for offset in range(tap_count):
        back_start = 2 * half_taps - offset
        back_doc = (doc_window[:, back_start : back_start + tok_count] == own_docs).astype(
            jnp.float32
        )[..., None]
        grad_conv_value = (
            grad_conv_value
            + tap_weights[:, offset]
            * grad_rims[:, back_start : back_start + tok_count].astype(jnp.float32)
            * back_doc
        )
    block_len = math.gcd(tok_count, 128)
    block_count = tok_count // block_len
    span = block_len + 2 * half_taps
    value_blocks = jnp.stack(
        [
            value_rims[:, index * block_len : index * block_len + span]
            for index in range(block_count)
        ],
        axis=1,
    )
    doc_blocks = jnp.stack(
        [
            doc_window[:, index * block_len : index * block_len + span]
            for index in range(block_count)
        ],
        axis=1,
    )
    own_blocks = own_docs.reshape(row_count, block_count, block_len)
    same_blocks = (own_blocks[..., :, None] == doc_blocks[..., None, :]).astype(jnp.float32)
    grad_blocks = grad_context.reshape(row_count, block_count, block_len, head_count, head_dim)
    value_heads = value_blocks.reshape(row_count, block_count, span, head_count, head_dim)
    pair_scores = jnp.einsum(
        "rbthe,rbshe->rbhts", grad_blocks, value_heads, preferred_element_type=jnp.float32
    )
    pair_scores = pair_scores * same_blocks[:, :, None, :, :]
    place_t = jnp.arange(block_len, dtype=jnp.int32)[:, None, None]
    place_s = jnp.arange(span, dtype=jnp.int32)[None, :, None]
    place_o = jnp.arange(tap_count, dtype=jnp.int32)[None, None, :]
    selector = (place_s - place_t == place_o).astype(jnp.float32)
    grad_conv = jnp.einsum("rbhts,tso->ho", pair_scores, selector, precision=highest)
    grad_values = (
        (
            grad_value_three.reshape(flat_rows, local_width)
            + grad_conv_value.reshape(flat_rows, local_width)
        )
        * keep_flat
    ).astype(jnp.bfloat16)
    grad_wq = left_product(x_flat, grad_queries)
    grad_wk = left_product(x_flat, grad_keys)
    grad_wv = left_product(x_flat, grad_values)
    input_part = (
        right_product(grad_queries, w_query)
        + right_product(grad_keys, w_key)
        + right_product(grad_values, w_value)
    )
    mp_width = model_width // lax.axis_size("mp")
    grad_in_local = lax.psum_scatter(input_part, "mp", scatter_dimension=1, tiled=True)
    grad_inputs = (
        (
            grad_in_local
            + lax.dynamic_slice_in_dim(grad_h1, lax.axis_index("mp") * mp_width, mp_width, 1)
        )
        .astype(jnp.bfloat16)
        .reshape(row_count, tok_count, mp_width)
    )
    weight_terms = (grad_wq, grad_wk, grad_wv, grad_out_w, grad_up, grad_down)
    row_summed = (
        lax.psum_scatter(weight_terms[0], "dp", scatter_dimension=0, tiled=True),
        lax.psum_scatter(weight_terms[1], "dp", scatter_dimension=0, tiled=True),
        lax.psum_scatter(weight_terms[2], "dp", scatter_dimension=0, tiled=True),
        lax.psum_scatter(weight_terms[3], "dp", scatter_dimension=1, tiled=True),
        lax.psum_scatter(weight_terms[4], "dp", scatter_dimension=0, tiled=True),
        lax.psum_scatter(weight_terms[5], "dp", scatter_dimension=1, tiled=True),
    )
    sum_q, sum_k, sum_v, sum_o, sum_up, sum_down = (
        lax.psum_scatter(row_summed[0], "seq", scatter_dimension=0, tiled=True),
        lax.psum_scatter(row_summed[1], "seq", scatter_dimension=0, tiled=True),
        lax.psum_scatter(row_summed[2], "seq", scatter_dimension=0, tiled=True),
        lax.psum_scatter(row_summed[3], "seq", scatter_dimension=1, tiled=True),
        lax.psum_scatter(row_summed[4], "seq", scatter_dimension=0, tiled=True),
        lax.psum_scatter(row_summed[5], "seq", scatter_dimension=1, tiled=True),
    )
    taps_total, norm_total = lax.psum(
        (grad_conv, jnp.stack([grad_gain_attn, grad_shift_attn, grad_gain_ffn, grad_shift_ffn])),
        ("dp", "seq"),
    )
    row_rms = jnp.sqrt(square_sums / (row_valid[:, None] * model_width) + 1e-06)
    return (
        outputs,
        grad_inputs,
        sum_q,
        sum_k,
        sum_v,
        sum_o,
        sum_up,
        sum_down,
        taps_total,
        norm_total[0],
        norm_total[1],
        norm_total[2],
        norm_total[3],
        row_rms,
    )


def solution(mesh):
    return jax.shard_map(
        shards,
        mesh=mesh,
        in_specs=(
            P("dp", "seq", None),
            P("dp", "seq", None),
            P("dp", None),
            P("dp", None),
            P(None, "mp"),
            P(None, "mp"),
            P(None, "mp"),
            P("mp", None),
            P(None, "mp"),
            P("mp", None),
            P("mp", None),
            P(),
            P(),
            P(),
            P(),
        ),
        out_specs=(
            P("dp", "seq", None),
            P("dp", "seq", "mp"),
            P(("dp", "seq"), "mp"),
            P(("dp", "seq"), "mp"),
            P(("dp", "seq"), "mp"),
            P("mp", ("dp", "seq")),
            P(("dp", "seq"), "mp"),
            P("mp", ("dp", "seq")),
            P("mp", None),
            P(),
            P(),
            P(),
            P(),
            P("dp", None),
        ),
        check_vma=False,
    )
```

profile of v0, /device:TPU:0, one launch (start us, length us, event | category | flops | bytes accessed | tf_op | source)
XLA Modules:
  0.0 1050.6 jit_solution(9677863473412820802)
XLA Ops:
  15.8 9.9 all_gather.6
  36.5 9.1 pmax.7
  73.2 11.5 %all_gather.7 = bf16[2,64,384]{2,1,0:T(8,128)(2,1)S(1)} all-gather(bf16[2,16,384]{2,1,0:T(8,128)(2,1)S(1)} %get-tuple-element.192), channel_id=1, replica_groups=mesh['dp'=4,'seq'=4,'mp'=2] {'seq'}, dimensions={1}, use_global_device_ids=true | all-gather | bytes 122880 | tf_op jit(solution)/shard_map/all_gather | solution.py:116
  103.8 9.6 psum.64
  135.1 51.7 %add_convert_fusion.6 = bf16[2,1024,384]{2,1,0:T(8,128)(2,1)} fusion(f32[2,1024,384]{2,1,0:T(8,128)} %copy.300, bf16[2,1024,384]{2,1,0:T(8,128)(2,1)} %bitcast.407, bf16[2,16,384]{2,1,0:T(8,128)(2,1)S(1)} %collective-permute-done.1, bf16[2,16,384]{2,1,0:T(8,128)(2,1)S(1)} %collective-permute-done, f32[2,1024]{1,0:T(2,128)S(1)} %get-tuple-element.183, ...), kind=kLoop, calls=%fused_computation.136 | loop fusion | flops 179306496 | bytes 6653440 | tf_op jit(solution)/shard_map/convert_element_type | solution.py:173
  186.9 5.9 fusion.237
  193.2 31.1 %all-reduce.16.cloned.1.call-done = f32[2048,768]{1,0:T(8,128)} async-done(((f32[2048,768]{1,0:T(8,128)}), f32[2048,768]{1,0:T(8,128)}) %all-reduce.16.cloned.1.call-update) | async-done | bytes 6291472 | tf_op jit(solution)/shard_map/psum | solution.py:174
  224.3 5.5 fusion.232
  232.5 33.6 %multiply_convert_fusion = (bf16[2048,1536]{1,0:T(8,128)(2,1)S(1)}, f32[2048,1536]{1,0:T(8,128)}, f32[2048,1536]{1,0:T(8,128)}) fusion(bf16[768,1536]{1,0:T(8,128)(2,1)S(1)} %copy-done, f32[2048,768]{1,0:T(8,128)S(1)} %get-tuple-element.134, f32[768]{0:T(1024)S(1)} %copy-done.232, f32[768]{0:T(1024)S(1)} %copy-done.173, f32[2048]{0:T(1024)S(1)} %fusion.184, ...), kind=kOutput, calls=%fused_computation.4 | convolution fusion | flops 5044174848 | bytes 40130560 | tf_op jit(solution)/shard_map/dot_general | solution.py:177
  268.8 6.8 fusion.238
  275.9 33.1 %all-reduce.18.cloned.1.call-done = f32[2048,768]{1,0:T(8,128)} async-done(((f32[2048,768]{1,0:T(8,128)}), f32[2048,768]{1,0:T(8,128)}) %all-reduce.18.cloned.1.call-update) | async-done | bytes 6291472 | tf_op jit(solution)/shard_map/psum | solution.py:180
  309.0 6.4 fusion.229
  325.4 17.8 %add_convert_fusion = bf16[2048,1536]{1,0:T(8,128)(2,1)} fusion(f32[2048,1536]{1,0:T(8,128)} %get-tuple-element.132, f32[2048,1536]{1,0:T(8,128)} %get-tuple-element.201, bf16[1536,768]{1,0:T(8,128)(2,1)} %param.24, f32[2048,768]{1,0:T(8,128)} %get-tuple-element.128, f32[2048]{0:T(1024)S(1)} %negate_multiply_fusion.2), kind=kOutput, calls=%fused_computation.3 | convolution fusion | flops 4879024128 | bytes 40116224 | tf_op jit(solution)/shard_map/dot_general | solution.py:60
  343.2 9.7 fusion.239
  353.8 32.6 %all-reduce.20.cloned.1.call-done = f32[2048,768]{1,0:T(8,128)} async-done(((f32[2048,768]{1,0:T(8,128)}), f32[2048,768]{1,0:T(8,128)}) %all-reduce.20.cloned.1.call-update) | async-done | bytes 6291472 | tf_op jit(solution)/shard_map/psum | solution.py:202
  386.4 8.6 multiply_reduce_fusion.4
  433.4 26.5 %multiply_add_fusion.1 = f32[2,1024,384]{2,1,0:T(8,128)} fusion(bf16[2,1024,384]{2,1,0:T(8,128)(2,1)S(1)} %bitcast.412, bf16[2,16,384]{2,1,0:T(8,128)(2,1)S(1)} %collective-permute-done.3, bf16[2,16,384]{2,1,0:T(8,128)(2,1)S(1)} %collective-permute-done.2, f32[2,1024]{1,0:T(2,128)S(1)} %copy-done.103, f32[384]{0:T(512)S(1)} %copy-done.185, ...), kind=kLoop, calls=%fused_computation.131 | loop fusion | flops 177733632 | bytes 5080576 | tf_op jit(solution)/shard_map/add | solution.py:302
  519.9 21.9 %reduce-scatter.24.cloned.1.call-done = f32[2,16,384]{2,1,0:T(8,128)} async-done(((f32[2,64,384]{2,1,0:T(8,128)}), f32[2,16,384]{2,1,0:T(8,128)}) %reduce-scatter.24.cloned.1.call-update) | async-done | bytes 49168 | tf_op jit(solution)/shard_map/reduce_scatter | solution.py:259
  547.0 6.3 reshape.408
  557.4 6.3 reshape.409
  563.7 10.7 %multiply_convert_fusion.1 = (bf16[2,1024,6,64]{1,3,2,0:T(8,128)(2,1)}, bf16[2,1024,6,64]{1,3,2,0:T(8,128)(2,1)S(1)}, bf16[2,1024,6,64]{1,3,2,0:T(8,128)(2,1)}) fusion(f32[2,1024,6,64]{1,3,2,0:T(8,128)} %convolution_bitcast_fusion, f32[2,1024,6,64]{1,3,2,0:T(8,128)} %bitcast.426, f32[2,1024]{1,0:T(2,128)S(1)} %copy-done.87, ...), kind=kLoop, calls=%fused_computation.127 | loop fusion | flops 7077888 | bytes 23601152 | tf_op jit(solution)/shard_map/convert_element_type | solution.py:343
  592.9 5.7 fusion.96
  598.6 10.7 %fusion.199 = f32[1536,768]{0,1:T(8,128)} fusion(bf16[2048,1536]{1,0:T(8,128)(2,1)} %copy-done.244, f32[2048,768]{1,0:T(8,128)} %get-tuple-element.128, f32[2048]{0:T(1024)S(1)} %copy-done.176), kind=kOutput, calls=%fused_computation.581 | convolution fusion | flops 4834983936 | bytes 17309696 | tf_op jit(solution)/shard_map/dot_general | solution.py:54
  610.0 12.4 %fusion.200 = f32[768,1536]{1,0:T(8,128)} fusion(bf16[2048,1536]{1,0:T(8,128)(2,1)} %add_convert_fusion, f32[2048,768]{1,0:T(8,128)} %copy-done.2, f32[768]{0:T(1024)S(1)} %copy-done.233, f32[768]{0:T(1024)S(1)} %copy-done.174, f32[2048]{0:T(1024)S(1)} %copy-done.93, f32[2048]{0:T(1024)S(1)} %broadcast_multiply_fusion.1), kind=kOutput, calls=%fused_computation.582 | convolution fusion | flops 4839702528 | bytes 17324032 | tf_op jit(solution)/shard_map/dot_general | solution.py:54
  657.9 6.5 fusion.15
  685.7 14.0 %reduce-scatter.30.cloned.1.call-done = f32[384,192]{0,1:T(8,128)} async-done(((f32[384,768]{0,1:T(8,128)}), f32[384,192]{0,1:T(8,128)}) %reduce-scatter.30.cloned.1.call-update) | async-done | bytes 294928 | tf_op jit(solution)/shard_map/reduce_scatter | solution.py:367
  700.9 85.0 %reduce-scatter.36.cloned.1.call-done = f32[1536,192]{0,1:T(8,128)} async-done(((f32[1536,768]{0,1:T(8,128)}), f32[1536,192]{0,1:T(8,128)}) %reduce-scatter.36.cloned.1.call-update) | async-done | bytes 1179664 | tf_op jit(solution)/shard_map/reduce_scatter | solution.py:369
  800.3 73.8 %reduce-scatter.32.cloned.1.call-done = f32[192,1536]{1,0:T(8,128)} async-done(((f32[768,1536]{1,0:T(8,128)}), f32[192,1536]{1,0:T(8,128)}) %reduce-scatter.32.cloned.1.call-update) | async-done | bytes 1179664 | tf_op jit(solution)/shard_map/reduce_scatter | solution.py:368
  878.5 9.9 psum.71
  895.9 74.5 %all-reduce.5 = (f32[6,33]{1,0:T(8,128)}, f32[4,768]{1,0:T(4,128)S(1)}) all-reduce(f32[6,33]{1,0:T(8,128)S(1)} %fusion.142, f32[4,768]{1,0:T(4,128)S(1)} %pad_maximum_fusion.4), channel_id=1, replica_groups=mesh['dp'=4,'seq'=4,'mp'=2] {'dp','seq'}, use_global_device_ids=true, to_apply=%region_47.48 | all-reduce | flops 3270 | bytes 26160 | tf_op jit(solution)/shard_map/psum | solution.py:379
  980.9 30.4 %reduce-scatter.38.cloned.1.call-done = f32[1536,48]{0,1:T(8,128)} async-done(((f32[1536,192]{0,1:T(8,128)}), f32[1536,48]{0,1:T(8,128)}) %reduce-scatter.38.cloned.1.call-update) | async-done | bytes 294928 | tf_op jit(solution)/shard_map/reduce_scatter | solution.py:377
  1011.3 32.2 %reduce-scatter.34.cloned.1.call-done = f32[48,1536]{1,0:T(8,128)} async-done(((f32[192,1536]{1,0:T(8,128)}), f32[48,1536]{1,0:T(8,128)}) %reduce-scatter.34.cloned.1.call-update) | async-done | bytes 294928 | tf_op jit(solution)/shard_map/reduce_scatter | solution.py:376
  (799 shorter events, 321.3 us)
Async XLA Ops:
  7.2 225.3 %copy-start = (bf16[768,1536]{1,0:T(8,128)(2,1)S(1)}, bf16[768,1536]{1,0:T(8,128)(2,1)}, u32[]{:S(2)}) copy-start(bf16[768,1536]{1,0:T(8,128)(2,1)} %param.23) | copy-start | bytes 7077892
  7.2 117.4 %all-reduce.14.cloned.1.call-start = ((), (), s32[]{:S(2)}) async-start(), calls=%async_computation.12 | async-start | bytes 786432 | tf_op jit(solution)/shard_map/psum | solution.py:145
  61.0 163.3 %all-reduce.16.cloned.1.call-start = ((), (), s32[]{:S(2)}) async-start(), calls=%async_computation.13 | async-start | bytes 12582912 | tf_op jit(solution)/shard_map/psum | solution.py:174
  62.5 71.9 %collective-permute-start = (bf16[2,16,384]{2,1,0:T(8,128)(2,1)}, bf16[2,16,384]{2,1,0:T(8,128)(2,1)S(1)}, u32[]{:S(2)}, u32[]{:S(2)}) collective-permute-start(bf16[2,16,384]{2,1,0:T(8,128)(2,1)} %get-tuple-element.150), channel_id=1, source_target_pairs={{0,2},{2,4},{4,6},{1,3},{3,5},{5,7},{8,10},{10,12},{12,14},{9,11},... | collective-permute-start | bytes 73736 | tf_op jit(solution)/shard_map/ppermute | solution.py:23
  64.9 69.5 %collective-permute-start.1 = (bf16[2,16,384]{2,1,0:T(8,128)(2,1)}, bf16[2,16,384]{2,1,0:T(8,128)(2,1)S(1)}, u32[]{:S(2)}, u32[]{:S(2)}) collective-permute-start(bf16[2,16,384]{2,1,0:T(8,128)(2,1)} %get-tuple-element.151), channel_id=1, source_target_pairs={{2,0},{4,2},{6,4},{3,1},{5,3},{7,5},{10,8},{12,10},{14,12},{11,9},... | collective-permute-start | bytes 73736 | tf_op jit(solution)/shard_map/ppermute | solution.py:24
  192.8 116.3 %all-reduce.18.cloned.1.call-start = ((), (), s32[]{:S(2)}) async-start(), calls=%async_computation.14 | async-start | bytes 12582912 | tf_op jit(solution)/shard_map/psum | solution.py:180
  232.5 162.5 %copy-start.92 = (f32[2048]{0:T(1024)}, f32[2048]{0:T(1024)S(1)}, u32[]{:S(2)}) copy-start(f32[2048]{0:T(1024)S(1)} %fusion.184) | copy-start | bytes 24580
  275.7 110.7 %all-reduce.20.cloned.1.call-start = ((), (), s32[]{:S(2)}) async-start(), calls=%async_computation.15 | async-start | bytes 12582912 | tf_op jit(solution)/shard_map/psum | solution.py:202
  353.0 111.2 %all-reduce.22.cloned.1.call-start = ((), (), s32[]{:S(2)}) async-start(), calls=%async_computation.16 | async-start | bytes 786432 | tf_op jit(solution)/shard_map/psum | solution.py:214
  418.8 101.1 %reduce-scatter.26.cloned.1.call-start = ((), (), s32[]{:S(2)}) async-start(), calls=%async_computation.18 | async-start | bytes 245760 | tf_op jit(solution)/shard_map/reduce_scatter | solution.py:265
  425.2 7.8 collective-permute-start.2
  426.5 6.5 collective-permute-start.3
  432.9 108.8 %reduce-scatter.24.cloned.1.call-start = ((), (), s32[]{:S(2)}) async-start(), calls=%async_computation.17 | async-start | bytes 245760 | tf_op jit(solution)/shard_map/reduce_scatter | solution.py:259
  515.3 153.6 %reduce-scatter.40.cloned.1.call-start = ((), (), s32[]{:S(2)}) async-start(), calls=%async_computation.25 | async-start | bytes 1474560
  579.4 91.5 %reduce-scatter.42.cloned.1.call-start = ((), (), s32[]{:S(2)}) async-start(), calls=%async_computation.26 | async-start | bytes 1474560
  585.9 86.8 %reduce-scatter.44.cloned.1.call-start = ((), (), s32[]{:S(2)}) async-start(), calls=%async_computation.27 | async-start | bytes 1474560
  592.7 107.0 %reduce-scatter.30.cloned.1.call-start = ((), (), s32[]{:S(2)}) async-start(), calls=%async_computation.20 | async-start | bytes 1474560 | tf_op jit(solution)/shard_map/reduce_scatter | solution.py:367
  598.5 187.4 %reduce-scatter.36.cloned.1.call-start = ((), (), s32[]{:S(2)}) async-start(), calls=%async_computation.23 | async-start | bytes 5898240 | tf_op jit(solution)/shard_map/reduce_scatter | solution.py:369
  609.3 264.8 %reduce-scatter.32.cloned.1.call-start = ((), (), s32[]{:S(2)}) async-start(), calls=%async_computation.21 | async-start | bytes 5898240 | tf_op jit(solution)/shard_map/reduce_scatter | solution.py:368
  622.4 348.6 %all-reduce.24.cloned.1.call-start = ((), (), s32[]{:S(2)}) async-start(), calls=%async_computation.29 | async-start | bytes 2359296
  674.7 302.0 %reduce-scatter.28.cloned.1.call-start = ((), (), s32[]{:S(2)}) async-start(), calls=%async_computation.19 | async-start | bytes 9437184 | tf_op jit(solution)/shard_map/reduce_scatter | solution.py:353
  683.2 103.1 %copy-start.241 = (u32[32]{0:T(128)S(1)}, u32[32]{0:T(128)}, u32[]{:S(2)}) copy-start(u32[32]{0:T(128)} %constant.143) | copy-start | bytes 388
  683.2 105.0 %copy-start.94 = (s32[2,4096]{1,0:T(2,128)S(1)}, s32[2,4096]{1,0:T(2,128)}, u32[]{:S(2)}) copy-start(s32[2,4096]{1,0:T(2,128)} %param.17) | copy-start | bytes 98308
  683.2 297.7 %reduce-scatter.46.cloned.1.call-start = ((), (), s32[]{:S(2)}) async-start(), calls=%async_computation.28 | async-start | bytes 368640
  699.7 93.6 %copy-start.7 = (bf16[2048,384]{1,0:T(8,128)(2,1)S(1)}, bf16[2048,384]{1,0:T(8,128)(2,1)}, u32[]{:S(2)}) copy-start(bf16[2048,384]{1,0:T(8,128)(2,1)} %fusion.29) | copy-start | bytes 4718596
  699.7 93.6 %copy-start.96 = (bf16[2,16,384]{2,1,0:T(8,128)(2,1)S(1)}, bf16[2,16,384]{2,1,0:T(8,128)(2,1)}, u32[]{:S(2)}) copy-start(bf16[2,16,384]{2,1,0:T(8,128)(2,1)} %copy-done.95) | copy-start | bytes 73732
  699.7 93.6 %copy-start.98 = (bf16[2,16,384]{2,1,0:T(8,128)(2,1)S(1)}, bf16[2,16,384]{2,1,0:T(8,128)(2,1)}, u32[]{:S(2)}) copy-start(bf16[2,16,384]{2,1,0:T(8,128)(2,1)} %copy-done.97) | copy-start | bytes 73732
  699.7 311.6 %reduce-scatter.38.cloned.1.call-start = ((), (), s32[]{:S(2)}) async-start(), calls=%async_computation.24 | async-start | bytes 1474560 | tf_op jit(solution)/shard_map/reduce_scatter | solution.py:377
  786.0 257.5 %reduce-scatter.34.cloned.1.call-start = ((), (), s32[]{:S(2)}) async-start(), calls=%async_computation.22 | async-start | bytes 1474560 | tf_op jit(solution)/shard_map/reduce_scatter | solution.py:376
  797.2 91.9 %copy-start.9 = (bf16[2048,384]{0,1:T(8,128)(2,1)S(1)}, bf16[2048,384]{0,1:T(8,128)(2,1)}, u32[]{:S(2)}) copy-start(bf16[2048,384]{0,1:T(8,128)(2,1)} %copy.301) | copy-start | bytes 4718596
  798.0 91.1 %copy-start.225 = (f32[768]{0:T(1024)S(1)}, f32[768]{0:T(1024)}, u32[]{:S(2)}) copy-start(f32[768]{0:T(1024)} %get-tuple-element.70) | copy-start | bytes 9220
  798.0 91.1 %copy-start.224 = (f32[768]{0:T(1024)S(1)}, f32[768]{0:T(1024)}, u32[]{:S(2)}) copy-start(f32[768]{0:T(1024)} %get-tuple-element.74) | copy-start | bytes 9220
  (237 other events, 2228.4 us)
Sparse Core Ops, SparseCore 0:
  61.2 44.4 all-reduce.13
  192.9 31.4 all-reduce.15
  275.8 33.1 all-reduce.17
  353.1 33.2 all-reduce.19
  418.9 45.2 all-reduce.21
  467.6 23.9 reduce-scatter.25
  515.4 26.3 reduce-scatter.23
  579.5 29.1 reduce-scatter.39
  611.2 27.9 reduce-scatter.41
  641.4 27.8 reduce-scatter.43
  671.7 27.9 reduce-scatter.29
  701.9 83.9 reduce-scatter.35
  788.3 85.7 reduce-scatter.31
  877.7 55.8 all-reduce.23
  935.8 14.4 reduce-scatter.27
  953.7 25.3 reduce-scatter.45
  982.7 28.5 reduce-scatter.37
  1014.9 28.5 reduce-scatter.33
where the time goes:
time: 1060 us; the launch traced here: 1050 us
  waiting for transfers between devices  355 us (33%)
  matrix products  233 us (22%)
  other arithmetic  158 us (15%)
  local copies, waits for them, and re-layouts  150 us (14%)
  blocking collectives  125 us (12%)
  between operations  19.5 us (2%)
  starting transfers between devices  12 us (1%)
    reduce_scatter x1, waiting for transfers between devices, shards(): lax.psum_scatter(weight_terms[5], 'dp', scatter_dimension=1, tiled=True)  85 us
    psum x1, blocking collectives, shards(): lax.psum((grad_conv, jnp.stack([grad_gain_attn, grad_shift_attn, grad_gai...  74.5 us
    reduce_scatter x1, waiting for transfers between devices, shards(): lax.psum_scatter(weight_terms[4], 'dp', scatter_dimension=0, tiled=True)  73.8 us
    convert_element_type x1, other arithmetic, shards(): (attended + conv_sum).astype(jnp.bfloat16).reshape(flat_rows, local_width)  51.7 us
    unnamed x534, local copies, waits for them, and re-layouts  51.2 us
    dot_general x6, matrix products, right_product(): lax.dot_general(left, right, (((1,), (1,)), ((), ())), preferred_element_...  40.3 us
    dot_general x1, matrix products, shards(): up_rows = jnp.dot(normed_low, w_up, preferred_element_type=jnp.float32)  33.6 us
    psum x1, waiting for transfers between devices, shards(): lax.psum(jnp.dot(act_low, w_down, preferred_element_type=jnp.float32), 'mp')  33.1 us
  transfers between devices with their start and end apart: 22, of which 10 were waited for; matrix products, arithmetic and copies ran while one was open for 26% of the time, Pallas kernels for 0%

commit v1 on v0

v1 whole, which is shorter than its diff:
```python
import functools

import jax
import jax.numpy as jnp
from jax import lax
from jax.experimental import pallas as pl
from jax.experimental.pallas import tpu as pltpu
from jax.sharding import PartitionSpec as P

M = 64
ITERS = 6
LEN = 4096
QUAD = 256
MESH = pl.DeviceIdType.MESH
F32 = jnp.float32
BF = jnp.bfloat16
EPS = 1e-05


def nn(a, b):
    return lax.dot_general(a, b, (((1,), (0,)), ((), ())), preferred_element_type=F32)


def nt(a, b):
    return lax.dot_general(a, b, (((1,), (1,)), ((), ())), preferred_element_type=F32)


def tn(a, b):
    return lax.dot_general(a, b, (((0,), (0,)), ((), ())), preferred_element_type=F32)


def split(a):
    high = a.astype(BF)
    return high, (a - high.astype(F32)).astype(BF)


def three(dot, a, b):
    ah, al = split(a)
    bh, bl = split(b)
    return dot(ah, bh) + (dot(ah, bl) + dot(al, bh))


def iota(shape, dim):
    return lax.broadcasted_iota(jnp.int32, shape, dim)


def block_mask():
    return iota((QUAD, QUAD), 0) // M == iota((QUAD, QUAD), 1) // M


def spread_blocks(x, mask):
    return jnp.where(mask, jnp.concatenate([x] * (QUAD // M), axis=0), jnp.zeros((), x.dtype))


def gather_blocks(y):
    lane = iota((M, QUAD), 1) // M
    out = jnp.zeros((M, QUAD), y.dtype)
    for h in range(QUAD // M):
        out = out + jnp.where(lane == h, y[h * M : (h + 1) * M], 0.0)
    return out


def params(limit=56, **kw):
    return pltpu.CompilerParams(vmem_limit_bytes=limit * 1024 * 1024, **kw)


def whole(shape):
    nd = len(shape)
    return pl.BlockSpec(shape, lambda *a: (0,) * nd)


def sds(shape, dtype):
    return jax.ShapeDtypeStruct(shape, dtype)


def valid_count(pad_ref, idx_ref):
    row = pad_ref[pl.ds(idx_ref[0], 1), :].astype(F32)
    return jnp.sum(row, axis=1, keepdims=True).astype(jnp.int32)


def project_kernel(
    idx, x_ref, pad_ref, q0, q1, k0, k1, v0, v1, q_ref, k_ref, v_ref, pack_ref, sums, *, tok
):
    step = pl.program_id(0)
    rows = x_ref.shape[1]
    half = q0.shape[1]
    x = x_ref[0]
    keep_n = valid_count(pad_ref, idx) - idx[1] * tok - step * rows
    keep = (iota((rows, 1), 0) < keep_n).astype(F32)
    marks = rows // M
    count = jnp.maximum(jnp.sum(keep.reshape(marks, M, 1), axis=1), 1.0)

    def one(w0, w1, out, place):
        for part, w in ((0, w0), (1, w1)):
            val = nn(x, w[...]).astype(BF)
            cols = pl.ds(part * half, half)
            if place is None:
                val = (val.astype(F32) * keep).astype(BF)
            out[:, cols] = val
            if place is not None:
                wide = (val.astype(F32) * keep).reshape(marks, M, half)
                sums[pl.ds(pl.multiple_of(place * (tok // M) + step * marks, marks), marks), cols] = (
                    jnp.sum(wide, axis=1) / count
                )

    one(q0, q1, q_ref, 0)
    one(k0, k1, k_ref, 1)
    one(v0, v1, v_ref, None)
    lm = tok // M

    @pl.when(step == 0)
    def _():
        pack_ref[2 * lm : 2 * lm + 16, :] = v_ref[0:16, :]

    @pl.when(step == pl.num_programs(0) - 1)
    def _():
        pack_ref[0 : 2 * lm, :] = sums[...].astype(BF)
        pack_ref[2 * lm + 16 : 2 * lm + 32, :] = v_ref[rows - 16 : rows, :]


def project(idx, inputs, padding, weights, tok):
    d = inputs.shape[2]
    half = weights[0].shape[1]
    rows = 512
    lm = tok // M
    cost = pl.CostEstimate(flops=6 * tok * d * d, bytes_accessed=12 * tok * d, transcendentals=0)
    return pl.pallas_call(
        functools.partial(project_kernel, tok=tok),
        grid_spec=pltpu.PrefetchScalarGridSpec(
            num_scalar_prefetch=1,
            grid=(tok // rows,),
            in_specs=[
                pl.BlockSpec((1, rows, d), lambda i, s: (s[0], i, 0)),
                whole(padding.shape),
            ]
            + [whole((d, half))] * 6,
            out_specs=[pl.BlockSpec((rows, d), lambda i, s: (i, 0))] * 3
            + [whole((2 * lm + 32, d))],
            scratch_shapes=[pltpu.VMEM((2 * lm, d), F32)],
        ),
        out_shape=[sds((tok, d), BF)] * 3 + [sds((2 * lm + 32, d), BF)],
        compiler_params=params(),
        cost_estimate=cost,
        name="project",
    )(idx, inputs, padding, *weights)


def enter(n):
    me = lax.axis_index("seq")
    barrier = pltpu.get_barrier_semaphore()
    for p in range(1, n):
        pl.semaphore_signal(
            barrier, inc=1, device_id={"seq": lax.rem(me + p, n)}, device_id_type=MESH
        )
    pl.semaphore_wait(barrier, n - 1)
    return me


def gather_kernel(*refs, n, count, edges):
    ins = refs[:count]
    outs = refs[count : 2 * count]
    at = 2 * count
    if edges:
        edge_in, edge_out = refs[at], refs[at + 1]
        at += 2
    send, recv, local = refs[at : at + 3]
    me = enter(n)
    copies = []
    slot = 0
    for src, dst in zip(ins, outs):
        for p in range(1, n):
            copies.append(
                pltpu.make_async_remote_copy(
                    src_ref=src,
                    dst_ref=dst.at[me],
                    send_sem=send.at[slot],
                    recv_sem=recv.at[slot],
                    device_id={"seq": lax.rem(me + p, n)},
                    device_id_type=MESH,
                )
            )
            slot += 1
    if edges:
        for side, p in ((0, 1), (1, n - 1)):
            first = 16 if side == 0 else 0
            copies.append(
                pltpu.make_async_remote_copy(
                    src_ref=edge_in.at[pl.ds(first, 16)],
                    dst_ref=edge_out.at[pl.ds(side * 16, 16)],
                    send_sem=send.at[slot],
                    recv_sem=recv.at[slot],
                    device_id={"seq": lax.rem(me + p, n)},
                    device_id_type=MESH,
                )
            )
            slot += 1
    for c in copies:
        c.start()
    locals_ = [
        pltpu.make_async_copy(src, dst.at[me], local.at[i])
        for i, (src, dst) in enumerate(zip(ins, outs))
    ]
    for c in locals_:
        c.start()
    for c in locals_:
        c.wait()
    for c in copies:
        c.wait()


def gather_seq(n, arrays, edge, cid):
    count = len(arrays)
    total = count * (n - 1) + (2 if edge is not None else 0)
    outs = [sds((n,) + a.shape, a.dtype) for a in arrays]
    args = list(arrays)
    if edge is not None:
        outs.append(sds(edge.shape, edge.dtype))
        args.append(edge)

    def body(*refs):
        ins = refs[: len(args)]
        rest = refs[len(args) :]
        o = rest[: len(outs)]
        sems = rest[len(outs) :]
        if edge is not None:
            order = ins[:count] + o[:count] + (ins[count], o[count]) + sems
        else:
            order = ins + o + sems
        gather_kernel(*order, n=n, count=count, edges=edge is not None)

    return pl.pallas_call(
        body,
        in_specs=[pl.BlockSpec(memory_space=pl.ANY)] * len(args),
        out_specs=[pl.BlockSpec(memory_space=pl.ANY)] * len(outs),
        out_shape=outs,
        scratch_shapes=[
            pltpu.SemaphoreType.DMA((total,)),
            pltpu.SemaphoreType.DMA((total,)),
            pltpu.SemaphoreType.DMA((count,)),
        ],
        compiler_params=params(8, collective_id=cid, has_side_effects=True),
        name="gather%d" % cid,
    )(*args)


def scatter_seq(n, array, cid):
    def body(src, dst, send, recv, local):
        me = enter(n)
        copies = []
        for p in range(1, n):
            to = lax.rem(me + p, n)
            copies.append(
                pltpu.make_async_remote_copy(
                    src_ref=src.at[to],
                    dst_ref=dst.at[me],
                    send_sem=send.at[p],
                    recv_sem=recv.at[p],
                    device_id={"seq": to},
                    device_id_type=MESH,
                )
            )
        for c in copies:
            c.start()
        own = pltpu.make_async_copy(src.at[me], dst.at[me], local)
        own.start()
        own.wait()
        for c in copies:
            c.wait()

    return pl.pallas_call(
        body,
        in_specs=[pl.BlockSpec(memory_space=pl.ANY)],
        out_specs=pl.BlockSpec(memory_space=pl.ANY),
        out_shape=sds(array.shape, array.dtype),
        scratch_shapes=[
            pltpu.SemaphoreType.DMA((n,)),
            pltpu.SemaphoreType.DMA((n,)),
            pltpu.SemaphoreType.DMA,
        ],
        compiler_params=params(8, collective_id=cid, has_side_effects=True),
        name="scatter%d" % cid,
    )(array)


def score_kernel(idx, q_ref, k_ref, v_ref, marks_ref, pad_ref, k1_ref, e_ref, mix_ref, stat_ref, *, tok):
    quad = pl.program_id(0)
    n = marks_ref.shape[0]
    lm = tok // M
    mask = block_mask()
    qm = jnp.concatenate([marks_ref[i, 0:lm, :] for i in range(n)], axis=0)
    km = jnp.concatenate([marks_ref[i, lm : 2 * lm, :] for i in range(n)], axis=0)
    s1 = nt(spread_blocks(km, mask), q_ref[...]) * 0.125
    s1 = s1.reshape(QUAD // M, M, tok)
    e1 = jnp.exp(s1 - jnp.max(s1, axis=1, keepdims=True))
    k1 = e1 / jnp.sum(e1, axis=1, keepdims=True)
    k1_ref[...] = k1.reshape(QUAD, tok).astype(BF)
    keep_n = valid_count(pad_ref, idx) - idx[1] * tok
    minus = jnp.where(iota((1, tok), 1) < keep_n, 0.0, 1000000000.0)
    s3 = nt(spread_blocks(qm, mask), k_ref[...]) * 0.125 - minus
    top = jnp.max(s3, axis=1, keepdims=True)
    e3 = jnp.exp(s3 - top)
    total = jnp.sum(e3, axis=1, keepdims=True)
    e3 = e3.astype(BF)
    e_ref[...] = e3
    mix_ref[...] = gather_blocks(nn(e3, v_ref[...])).astype(BF)
    lane = iota((M, 128), 1)
    stat = jnp.where(quad == 0, jnp.zeros((M, 128), F32), stat_ref[...])
    for h in range(QUAD // M):
        stat = jnp.where(lane == quad * (QUAD // M) + h, top[h * M : (h + 1) * M], stat)
        stat = jnp.where(lane == 64 + quad * (QUAD // M) + h, total[h * M : (h + 1) * M], stat)
    stat_ref[...] = stat


def scores(idx, q, k, v, marks, padding):
    tok, d = q.shape
    n = marks.shape[0]
    lane = lambda i, s: (0, i)
    cost = pl.CostEstimate(
        flops=6 * tok * d * QUAD, bytes_accessed=10 * tok * d, transcendentals=2 * tok * d
    )
    return pl.pallas_call(
        functools.partial(score_kernel, tok=tok),
        grid_spec=pltpu.PrefetchScalarGridSpec(
            num_scalar_prefetch=1,
            grid=(d // QUAD,),
            in_specs=[pl.BlockSpec((tok, QUAD), lane)] * 3
            + [pl.BlockSpec((n, marks.shape[1], QUAD), lambda i, s: (0, 0, i)), whole(padding.shape)],
            out_specs=[pl.BlockSpec((QUAD, tok), lambda i, s: (i, 0))] * 2
            + [pl.BlockSpec((M, QUAD), lane), whole((M, 128))],
        ),
        out_shape=[sds((d, tok), BF), sds((d, tok), BF), sds((M, d), BF), sds((M, 128), F32)],
        compiler_params=params(),
        cost_estimate=cost,
        name="scores",
    )(idx, q, k, v, marks, padding)


def pinv_kernel(idx, marks_ref, k2_ref, inv_ref, save_ref, *, lm):
    n = marks_ref.shape[0]
    d = marks_ref.shape[2]
    quads = d // QUAD
    mask = block_mask()
    ident = (iota((QUAD, QUAD), 0) == iota((QUAD, QUAD), 1)).astype(F32)
    qm = jnp.concatenate([marks_ref[i, 0:lm, :] for i in range(n)], axis=0)
    km = jnp.concatenate([marks_ref[i, lm : 2 * lm, :] for i in range(n)], axis=0)
    kernel, z = [], []
    for c in range(quads):
        cols = slice(c * QUAD, (c + 1) * QUAD)
        s2 = nt(spread_blocks(qm[:, cols], mask), spread_blocks(km[:, cols], mask)) * 0.125
        s2 = jnp.where(mask, s2, -1e30)
        e2 = jnp.exp(s2 - jnp.max(s2, axis=1, keepdims=True))
        e2 = e2 / jnp.sum(e2, axis=1, keepdims=True)
        kernel.append(e2)
        sums = jnp.sum(e2, axis=0, keepdims=True)
        lane = iota((1, QUAD), 1) // M
        scale = jnp.zeros((1, QUAD), F32)
        for h in range(QUAD // M):
            best = jnp.max(jnp.where(lane == h, sums, 0.0), axis=1, keepdims=True)
            scale = jnp.where(lane == h, 1.0 / best, scale)
        z.append(e2.T * scale)
        k2_ref[:, cols] = gather_blocks(e2)
    sel = jnp.minimum(idx[1], quads - 1)

    def keep(it, kind, vals):
        if kind is None:
            return
        for c in range(quads):

            @pl.when(sel == c)
            def _():
                save_ref[it, kind] = vals[c].astype(BF)

    ksp = [split(a) for a in kernel]

    def mul(a, b):
        return nn(a[0], b[0]) + (nn(a[0], b[1]) + nn(a[1], b[0]))

    for it in range(ITERS):
        zs = [split(a) for a in z]
        p = [mul(a, b) for a, b in zip(ksp, zs)]
        ps = [split(a) for a in p]
        i2 = [15.0 * ident - mul(a, split(7.0 * ident - b)) for a, b in zip(ps, p)]
        i3 = [13.0 * ident - mul(a, split(b)) for a, b in zip(ps, i2)]
        keep(it, 0, z)
        keep(it, 1, p)
        keep(it, 2, i2)
        keep(it, 3, i3)
        z = [0.25 * mul(a, split(b)) for a, b in zip(zs, i3)]
    for c in range(quads):
        inv_ref[:, c * QUAD : (c + 1) * QUAD] = gather_blocks(z[c])


def pinv(idx, marks, lm):
    d = marks.shape[2]
    shape = (ITERS, 4, QUAD, QUAD)
    cost = pl.CostEstimate(
        flops=24 * 3 * 3 * 2 * QUAD**3, bytes_accessed=4 * 10**6, transcendentals=0
    )
    return pl.pallas_call(
        functools.partial(pinv_kernel, lm=lm),
        grid_spec=pltpu.PrefetchScalarGridSpec(
            num_scalar_prefetch=1,
            grid=(1,),
            in_specs=[whole(marks.shape)],
            out_specs=[whole((M, d)), whole((M, d)), whole(shape)],
        ),
        out_shape=[sds((M, d), F32), sds((M, d), F32), sds(shape, BF)],
        compiler_params=params(),
        cost_estimate=cost,
        name="pinv",
    )(idx, marks)


def per_head(stat, base, c):
    lane = iota((M, QUAD), 1) // M
    out = jnp.zeros((M, QUAD), F32)
    for h in range(QUAD // M):
        at = base + c * (QUAD // M) + h
        out = jnp.where(lane == h, stat[:, at : at + 1], out)
    return out


def combine_kernel(idx, mix_ref, stat_ref, inv_ref, cm_ref, lv_ref, gst_ref):
    n = mix_ref.shape[0]
    d = mix_ref.shape[2]
    lane = iota((M, 128), 1)
    top = stat_ref[0]
    for i in range(1, n):
        top = jnp.maximum(top, stat_ref[i])
    top = jnp.where(lane < 64, top, 0.0)
    total = jnp.zeros((M, 128), F32)
    scales = []
    for i in range(n):
        st = stat_ref[i]
        sc = jnp.where(lane < 64, jnp.exp(st - top), 0.0)
        scales.append(sc)
        total = total + sc * pltpu.roll(st, 64, 1)
    own = jnp.zeros((M, 128), F32)
    for i in range(n):
        own = jnp.where(idx[1] == i, scales[i], own)
    gst_ref[...] = jnp.where(lane < 64, own, pltpu.roll(total, 64, 1))
    mask = block_mask()
    for c in range(d // QUAD):
        cols = slice(c * QUAD, (c + 1) * QUAD)
        mixed = jnp.zeros((M, QUAD), F32)
        for i in range(n):
            mixed = mixed + per_head(scales[i], 0, c) * mix_ref[i, :, cols].astype(F32)
        lv = mixed / per_head(total, 0, c)
        lv_ref[:, cols] = lv
        cm = three(nn, spread_blocks(inv_ref[:, cols], mask), spread_blocks(lv, mask))
        cm_ref[:, cols] = gather_blocks(cm).astype(BF)


def combine(idx, mix, stat, inv):
    d = mix.shape[2]
    return pl.pallas_call(
        combine_kernel,
        grid_spec=pltpu.PrefetchScalarGridSpec(
            num_scalar_prefetch=1,
            grid=(1,),
            in_specs=[whole(mix.shape), whole(stat.shape), whole(inv.shape)],
            out_specs=[whole((M, d)), whole((M, d)), whole((M, 128))],
        ),
        out_shape=[sds((M, d), BF), sds((M, d), F32), sds((M, 128), F32)],
        compiler_params=params(),
        name="combine",
    )(idx, mix, stat, inv)


def doc_bounds(doc_ref, idx):
    row = doc_ref[pl.ds(idx[0], 1), :]
    return [
        jnp.sum((row < j).astype(F32), axis=1, keepdims=True).astype(jnp.int32)
        for j in range(1, 9)
    ]


def docs_at(place, bounds, length):
    doc = jnp.zeros(place.shape, jnp.int32)
    for b in bounds:
        doc = doc + (place >= b).astype(jnp.int32)
    return jnp.where((place >= 0) & (place < length), doc, -1)


def fill_bands(taps_ref, band_ref, half, flip):
    heads, width = taps_ref.shape[0], 2 * half + 1
    rows, span = band_ref.shape[1], band_ref.shape[2]
    gap = iota((rows, span), 1) - iota((rows, span), 0) - 64
    if flip:
        gap = -gap
    for h in range(heads):
        acc = jnp.zeros((rows, span), F32)
        line = taps_ref[h : h + 1, :]
        for o in range(width):
            acc = jnp.where(gap == o - half, line[:, o : o + 1], acc)
        band_ref[h] = acc.astype(BF)


def banded(band_ref, window, same, col0):
    lane = iota((band_ref.shape[1], 128), 1)
    first = nn(band_ref[col0] * same, window)
    second = nn(band_ref[col0 + 1] * same, window)
    return jnp.where(lane < 64, first, second)


def fill_halo(ext, body, edge_ref, tok):
    ext[0:48, :] = jnp.zeros((48, ext.shape[1]), BF)
    ext[48:64, :] = edge_ref[0:16, :]
    ext[64 : 64 + tok, :] = body[...]
    ext[64 + tok : 80 + tok, :] = edge_ref[16:32, :]
    ext[80 + tok :, :] = jnp.zeros((48, ext.shape[1]), BF)


def erf_parts(u):
    a = jnp.abs(u) * 0.7071067811865476
    e = jnp.exp(-0.5 * u * u)
    t = 1.0 / (1.0 + 0.3275911 * a)
    poly = t * (
        0.254829592
        + t * (-0.284496736 + t * (1.421413741 + t * (-1.453152027 + t * 1.061405429)))
    )
    tail = 0.5 * poly * e
    cdf = jnp.where(u < 0.0, tail, 1.0 - tail)
    return cdf, e * 0.3989422804014327


def norm_stats(h):
    mean = jnp.mean(h, axis=-1, keepdims=True)
    centre = h - mean
    rstd = lax.rsqrt(jnp.mean(centre * centre, axis=-1, keepdims=True) + EPS)
    return centre * rstd, rstd


def norm_back(g, hat, rstd):
    return rstd * (
        g
        - jnp.mean(g, axis=-1, keepdims=True)
        - hat * jnp.mean(g * hat, axis=-1, keepdims=True)
    )


def forward_kernel(
    idx,
    x_ref,
    cot_ref,
    pad_ref,
    doc_ref,
    v_ref,
    edge_ref,
    k1_ref,
    cm_ref,
    taps_ref,
    wo0,
    wo1,
    wu0,
    wu1,
    wd0,
    wd1,
    ga_ref,
    sa_ref,
    gf_ref,
    sf_ref,
    out_ref,
    ctx_ref,
    h1_ref,
    nl_ref,
    act0,
    act1,
    gp0,
    gp1,
    gh2_ref,
    acc_ref,
    ext,
    band,
    *,
    tok,
):
    step = pl.program_id(0)
    rows, d = ctx_ref.shape
    half = wo0.shape[0]
    taps = taps_ref.shape[1]

    @pl.when(step == 0)
    def _():
        fill_halo(ext, v_ref, edge_ref, tok)
        fill_bands(taps_ref, band, taps // 2, False)
        acc_ref[...] = jnp.zeros_like(acc_ref)

    bounds = doc_bounds(doc_ref, idx)
    mask = block_mask()
    start = idx[1] * tok + step * rows
    parts = []
    for sub in range(rows // 128):
        place = start + sub * 128
        same = (
            docs_at(place + iota((128, 1), 0), bounds, LEN)
            == docs_at(place - 64 + iota((1, 256), 1), bounds, LEN)
        ).astype(BF)
        base = pl.multiple_of(step * rows + sub * 128, 128)
        cols = []
        for pair in range(d // 128):
            window = ext[pl.ds(base, 256), pair * 128 : (pair + 1) * 128]
            cols.append(banded(band, window, same, 2 * pair))
        parts.append(jnp.concatenate(cols, axis=1))
    conv = jnp.concatenate(parts, axis=0)
    for c in range(d // QUAD):
        cols = slice(c * QUAD, (c + 1) * QUAD)
        att = tn(k1_ref[cols, :], spread_blocks(cm_ref[:, cols], mask))
        ctx_ref[:, cols] = (att + conv[:, cols]).astype(BF)
    branch = nn(ctx_ref[:, :half], wo0[...]) + nn(ctx_ref[:, half:], wo1[...])
    xf = x_ref[0].astype(F32)
    h1 = xf + branch
    h1_ref[...] = h1
    hat1, _ = norm_stats(h1)
    normed = hat1 * ga_ref[...] + sa_ref[...]
    nl = normed.astype(BF)
    nl_ref[...] = nl
    ffn = jnp.zeros((rows, d), F32)
    chunk = 512
    for wu, wd, act, gp in ((wu0, wd0, act0, gp0), (wu1, wd1, act1, gp1)):
        for at in range(0, wu.shape[1], chunk):
            cols = slice(at, at + chunk)
            u = nn(nl, wu[:, cols])
            cdf, pdf = erf_parts(u)
            a = (u * cdf).astype(BF)
            act[:, cols] = a
            gp[:, cols] = (cdf + u * pdf).astype(BF)
            ffn = ffn + nn(a, wd[cols, :])
    hat2, rstd2 = norm_stats(normed + ffn)
    out_ref[...] = (hat2 * gf_ref[...] + sf_ref[...]).astype(BF)
    cot = cot_ref[0].astype(F32)
    gh2_ref[...] = norm_back(cot * gf_ref[...], hat2, rstd2)
    keep_n = valid_count(pad_ref, idx) - start
    keep = (iota((rows, 1), 0) < keep_n).astype(F32)
    acc_ref[0:1, :] += jnp.sum(cot * hat2, axis=0, keepdims=True)
    acc_ref[1:2, :] += jnp.sum(cot, axis=0, keepdims=True)
    acc_ref[2:3, :] += jnp.sum(xf * xf * keep, axis=0, keepdims=True)
    acc_ref[3:4, :] += jnp.sum(branch * branch * keep, axis=0, keepdims=True)
    acc_ref[4:5, :] += jnp.sum(ffn * ffn * keep, axis=0, keepdims=True)


def forward(idx, inputs, cot, padding, documents, v, edge, k1, cm, taps, wo, wu, wd, vecs):
    tok, d = v.shape
    rows = 256
    f2 = wu[0].shape[1]
    blk = lambda i, s: (i, 0)
    row = pl.BlockSpec((1, rows, d), lambda i, s: (s[0], i, 0))
    cost = pl.CostEstimate(
        flops=8 * tok * d * f2, bytes_accessed=60 * tok * d, transcendentals=4 * tok * f2
    )
    return pl.pallas_call(
        functools.partial(forward_kernel, tok=tok),
        grid_spec=pltpu.PrefetchScalarGridSpec(
            num_scalar_prefetch=1,
            grid=(tok // rows,),
            in_specs=[
                row,
                row,
                whole(padding.shape),
                whole(documents.shape),
                whole(v.shape),
                whole(edge.shape),
                pl.BlockSpec((d, rows), lambda i, s: (0, i)),
                whole(cm.shape),
                whole(taps.shape),
            ]
            + [whole(w.shape) for w in (*wo, *wu, *wd, *vecs)],
            out_specs=[pl.BlockSpec((rows, d), blk)] * 4
            + [pl.BlockSpec((rows, f2), blk)] * 4
            + [pl.BlockSpec((rows, d), blk), whole((8, d))],
            scratch_shapes=[
                pltpu.VMEM((tok + 128, d), BF),
                pltpu.VMEM((taps.shape[0], 128, 256), BF),
            ],
        ),
        out_shape=[sds((tok, d), BF), sds((tok, d), BF), sds((tok, d), F32), sds((tok, d), BF)]
        + [sds((tok, f2), BF)] * 4
        + [sds((tok, d), F32), sds((8, d), F32)],
        compiler_params=params(60),
        cost_estimate=cost,
        name="forward",
    )(idx, inputs, cot, padding, documents, v, edge, k1, cm, taps, *wo, *wu, *wd, *vecs)


def backward_kernel(
    idx, gh2_ref, h1_ref, gp0, gp1, wo0, wo1, wu0, wu1, wd0, wd1, ga_ref,
    du0, du1, gh1_ref, gc_ref, acc_ref,
):
    step = pl.program_id(0)
    half = wo0.shape[0]

    @pl.when(step == 0)
    def _():
        acc_ref[...] = jnp.zeros_like(acc_ref)

    gh2 = gh2_ref[...]
    low = gh2.astype(BF)
    gn = gh2
    chunk = 512
    for wu, wd, gp, du in ((wu0, wd0, gp0, du0), (wu1, wd1, gp1, du1)):
        for at in range(0, wu.shape[1], chunk):
            cols = slice(at, at + chunk)
            g = (nt(low, wd[cols, :]) * gp[:, cols].astype(F32)).astype(BF)
            du[:, cols] = g
            gn = gn + nt(g, wu[:, cols])
    hat1, rstd1 = norm_stats(h1_ref[...])
    acc_ref[0:1, :] += jnp.sum(gn * hat1, axis=0, keepdims=True)
    acc_ref[1:2, :] += jnp.sum(gn, axis=0, keepdims=True)
    gh1 = norm_back(gn * ga_ref[...], hat1, rstd1).astype(BF)
    gh1_ref[...] = gh1
    gc_ref[:, :half] = nt(gh1, wo0[...]).astype(BF)
    gc_ref[:, half:] = nt(gh1, wo1[...]).astype(BF)


def backward(idx, gh2, h1, gp, wo, wu, wd, ga):
    tok, d = h1.shape
    rows = 256
    f2 = wu[0].shape[1]
    blk = lambda i, s: (i, 0)
    cost = pl.CostEstimate(flops=8 * tok * d * f2, bytes_accessed=40 * tok * d, transcendentals=0)
    return pl.pallas_call(
        backward_kernel,
        grid_spec=pltpu.PrefetchScalarGridSpec(
            num_scalar_prefetch=1,
            grid=(tok // rows,),
            in_specs=[pl.BlockSpec((rows, d), blk)] * 2
            + [pl.BlockSpec((rows, f2), blk)] * 2
            + [whole(w.shape) for w in (*wo, *wu, *wd, ga)],
            out_specs=[pl.BlockSpec((rows, f2), blk)] * 2
            + [pl.BlockSpec((rows, d), blk)] * 2
            + [whole((8, d))],
        ),
        out_shape=[sds((tok, f2), BF)] * 2 + [sds((tok, d), BF)] * 2 + [sds((8, d), F32)],
        compiler_params=params(60),
        cost_estimate=cost,
        name="backward",
    )(idx, gh2, h1, *gp, *wo, *wu, *wd, ga)


def weight_kernel(idx, *refs, nl, nr, blocks, shape):
    lhs = refs[:nl]
    rhs = refs[nl : nl + nl * nr]
    outs = refs[nl + nl * nr : nl + nl * nr + nr]
    held = refs[-1]
    step = pl.program_id(0)
    z, sq, chunk = shape

    @pl.when(step == 0)
    def _():
        for i in range(nl):
            a = lhs[i][...] if len(lhs[i].shape) == 2 else lhs[i][0]
            tokens = a.shape[0]
            t = a.astype(BF).T
            if z == 0:
                held[:, i * tokens : (i + 1) * tokens] = t
            else:
                lhs_t = refs[-2]
                lhs_t[...] = t
                for b0 in range(2):
                    for b1 in range(2):
                        for zp in range(z):
                            place = ((b0 * 2 + b1) * z + zp) * chunk
                            src = (idx[2] ^ zp) * sq + (idx[1] ^ (b1 * 2 + b0))
                            held[place : place + chunk, i * tokens : (i + 1) * tokens] = lhs_t[
                                pl.ds(pl.multiple_of(src * chunk, chunk), chunk), :
                            ]

    tokens = held.shape[1] // nl
    for r in range(nr):
        acc = None
        for i in range(nl):
            part = nn(held[:, i * tokens : (i + 1) * tokens], rhs[i * nr + r][...])
            acc = part if acc is None else acc + part
        outs[r][...] = acc.astype(BF)


def weight_grads(idx, lhs, rhs, width, shape):
    nl, nr = len(lhs), len(rhs[0])
    tok, d = rhs[0][0].shape[0], lhs[0][0].shape[-1]
    cols = rhs[0][0].shape[1]
    blocks = cols // width
    in_specs, args = [], []
    for a, row in lhs:
        if a.ndim == 3:
            if row == 0:
                in_specs.append(pl.BlockSpec((1, tok, d), lambda j, s: (s[0], 0, 0)))
            else:
                in_specs.append(pl.BlockSpec((1, tok, d), lambda j, s: (1 - s[0], 0, 0)))
        else:
            in_specs.append(whole(a.shape))
        args.append(a)
    for group in rhs:
        for b in group:
            in_specs.append(pl.BlockSpec((tok, width), lambda j, s: (0, j)))
            args.append(b)
    cost = pl.CostEstimate(
        flops=2 * tok * d * cols * nl * nr, bytes_accessed=8 * tok * cols, transcendentals=0
    )
    return pl.pallas_call(
        functools.partial(weight_kernel, nl=nl, nr=nr, blocks=blocks, shape=shape),
        grid_spec=pltpu.PrefetchScalarGridSpec(
            num_scalar_prefetch=1,
            grid=(blocks,),
            in_specs=in_specs,
            out_specs=[pl.BlockSpec((d, width), lambda j, s: (0, j))] * nr,
            scratch_shapes=[pltpu.VMEM((d, tok), BF), pltpu.VMEM((d, tok * nl), BF)],
        ),
        out_shape=[sds((d, cols), BF)] * nr,
        compiler_params=params(60),
        cost_estimate=cost,
        name="weights",
    )(idx, *args)


def halving(seq_n, bit):
    return [(i, i ^ bit) for i in range(seq_n)]


def reduce_fast(full):
    seq_n, dp_n = lax.axis_size("seq"), lax.axis_size("dp")
    d, n = full.shape
    q = d // 4
    na = n // 2
    a, b = full[:, :na], full[:, na:]
    send_a, keep_a = a[2 * q :], a[: 2 * q]
    send_b = jnp.concatenate([b[q : 2 * q], b[3 * q :]], axis=0)
    keep_b = jnp.concatenate([b[:q], b[2 * q : 3 * q]], axis=0)
    got_a = lax.ppermute(send_a, "seq", halving(seq_n, 1))
    got_b = lax.ppermute(send_b, "seq", halving(seq_n, 2))
    add = lambda u, v: (u.astype(F32) + v.astype(F32)).astype(BF)
    a, b = add(keep_a, got_a), add(keep_b, got_b)
    got_a = lax.ppermute(a[q:], "seq", halving(seq_n, 2))
    got_b = lax.ppermute(b[q:], "seq", halving(seq_n, 1))
    c = jnp.concatenate([add(a[:q], got_a), add(b[:q], got_b)], axis=1)
    ch = q // dp_n
    out = c[:ch].astype(F32)
    for p in range(1, dp_n):
        out = out + lax.ppermute(c[p * ch : (p + 1) * ch], "dp", halving(dp_n, p)).astype(F32)
    return out


def reduce_any(full):
    part = lax.psum_scatter(full.astype(F32), "dp", scatter_dimension=0, tiled=True)
    return lax.psum_scatter(part, "seq", scatter_dimension=0, tiled=True)


def first_kernel(q_ref, k1_ref, gc_ref, cm_ref, marks_ref, gq_ref, mix_ref, km_ref, *, tok):
    n = marks_ref.shape[0]
    lm = tok // M
    mask = block_mask()
    km = spread_blocks(
        jnp.concatenate([marks_ref[i, lm : 2 * lm, :] for i in range(n)], axis=0), mask
    )
    gc = gc_ref[...]
    k1 = k1_ref[...]
    mix_ref[...] = gather_blocks(nn(k1, gc)).astype(BF)
    g = nt(spread_blocks(cm_ref[...], mask), gc).reshape(QUAD // M, M, tok)
    kf = k1.astype(F32).reshape(QUAD // M, M, tok)
    inner = jnp.sum(g * kf, axis=1, keepdims=True)
    g1 = (kf * (g - inner)).reshape(QUAD, tok).astype(BF)
    gq_ref[...] = (tn(g1, km) * 0.125).astype(BF)
    km_ref[...] = gather_blocks(nn(g1, q_ref[...])) * 0.125


def first_back(q, k1, gc, cm, marks):
    tok, d = q.shape
    n = marks.shape[0]
    lane = lambda i: (0, i)
    cost = pl.CostEstimate(flops=8 * tok * d * QUAD, bytes_accessed=8 * tok * d, transcendentals=0)
    return pl.pallas_call(
        functools.partial(first_kernel, tok=tok),
        grid=(d // QUAD,),
        in_specs=[
            pl.BlockSpec((tok, QUAD), lane),
            pl.BlockSpec((QUAD, tok), lambda i: (i, 0)),
            pl.BlockSpec((tok, QUAD), lane),
            pl.BlockSpec((M, QUAD), lane),
            pl.BlockSpec((n, marks.shape[1], QUAD), lambda i: (0, 0, i)),
        ],
        out_specs=[
            pl.BlockSpec((tok, QUAD), lane),
            pl.BlockSpec((M, QUAD), lane),
            pl.BlockSpec((M, QUAD), lane),
        ],
        out_shape=[sds((tok, d), BF), sds((M, d), BF), sds((M, d), F32)],
        compiler_params=params(),
        cost_estimate=cost,
        name="first_back",
    )(q, k1, gc, cm, marks)


def middle_kernel(idx, gmix_ref, lv_ref, inv_ref, gst_ref, gm_ref, gt_ref):
    n = gmix_ref.shape[0]
    d = lv_ref.shape[1]
    mask = block_mask()
    lane = iota((M, 128), 1)
    head = iota((M, QUAD), 1) // M
    stat = gst_ref[...]
    gt = jnp.zeros((M, 128), F32)
    for c in range(d // QUAD):
        cols = slice(c * QUAD, (c + 1) * QUAD)
        gmix = jnp.zeros((M, QUAD), F32)
        for i in range(n):
            gmix = gmix + gmix_ref[i, :, cols].astype(F32)
        glv = gather_blocks(
            three(tn, spread_blocks(inv_ref[:, cols], mask), spread_blocks(gmix, mask))
        )
        scale = per_head(stat, 0, c)
        total = per_head(stat, 64, c)
        gm_ref[:, cols] = ((glv / total).astype(BF).astype(F32) * scale).astype(BF)
        prod = glv * lv_ref[:, cols]
        for h in range(QUAD // M):
            at = c * (QUAD // M) + h
            s = jnp.sum(jnp.where(head == h, prod, 0.0), axis=1, keepdims=True)
            gt = jnp.where(lane == at, -s / stat[:, 64 + at : 65 + at] * stat[:, at : at + 1], gt)
    gt_ref[...] = gt


def middle(idx, gmix, lv, inv, gst):
    d = lv.shape[1]
    return pl.pallas_call(
        middle_kernel,
        grid_spec=pltpu.PrefetchScalarGridSpec(
            num_scalar_prefetch=1,
            grid=(1,),
            in_specs=[whole(gmix.shape), whole(lv.shape), whole(inv.shape), whole(gst.shape)],
            out_specs=[whole((M, d)), whole((M, 128))],
        ),
        out_shape=[sds((M, d), BF), sds((M, 128), F32)],
        compiler_params=params(),
        name="middle",
    )(idx, gmix, lv, inv, gst)


def pinv_back_kernel(idx, gmix_ref, lv_ref, k2_ref, save_ref, marks_ref, out_ref, *, lm):
    n = gmix_ref.shape[0]
    mask = block_mask()
    ident = (iota((QUAD, QUAD), 0) == iota((QUAD, QUAD), 1)).astype(F32)
    gmix = jnp.zeros((M, QUAD), F32)
    for i in range(n):
        gmix = gmix + gmix_ref[i].astype(F32)
    dz = three(nt, spread_blocks(gmix, mask), spread_blocks(lv_ref[...], mask))
    kernel = spread_blocks(k2_ref[...], mask)
    klow = kernel.astype(BF)
    dk = jnp.zeros((QUAD, QUAD), F32)
    ibf = ident.astype(BF)
    for it in range(ITERS - 1, -1, -1):
        z, p, i2, i3 = (save_ref[it, kind] for kind in range(4))
        i1 = 7.0 * ibf - p
        dlow = dz.astype(BF)
        d3 = (0.25 * tn(z, dlow)).astype(BF)
        dp = nt(d3, i2)
        d2 = (-tn(p, d3)).astype(BF)
        dp = dp + nt(d2, i1)
        d1 = -tn(p, d2)
        dp = (-dp - d1).astype(BF)
        dz = 0.25 * nt(dlow, i3) + tn(klow, dp)
        dk = dk + nt(dp, z)
    sums = jnp.sum(kernel, axis=0, keepdims=True)
    lane = iota((1, QUAD), 1) // M
    dzt = jnp.where(mask, dz, 0.0).T
    dsum = jnp.sum(dzt * kernel, axis=0, keepdims=True)
    scale = jnp.zeros((1, QUAD), F32)
    extra = jnp.zeros((1, QUAD), F32)
    for h in range(QUAD // M):
        mine = lane == h
        best = jnp.max(jnp.where(mine, sums, 0.0), axis=1, keepdims=True)
        dscale = jnp.sum(jnp.where(mine, dsum, 0.0), axis=1, keepdims=True)
        is_best = (mine & (sums == best)).astype(F32)
        share = is_best / jnp.sum(is_best, axis=1, keepdims=True)
        scale = jnp.where(mine, 1.0 / best, scale)
        extra = jnp.where(mine, -dscale / (best * best) * share, extra)
    dk = dk + dzt * scale + extra
    inner = jnp.sum(jnp.where(mask, dk * kernel, 0.0), axis=1, keepdims=True)
    g2 = kernel * (dk - inner)
    qm = jnp.concatenate([marks_ref[i, 0:lm, :] for i in range(n)], axis=0)
    km = jnp.concatenate([marks_ref[i, lm : 2 * lm, :] for i in range(n)], axis=0)
    g2h, g2l = split(g2)
    kb, qb = spread_blocks(km, mask), spread_blocks(qm, mask)
    use = (idx[1] < idx[3]).astype(F32) * 0.125
    out_ref[0] = gather_blocks(nn(g2h, kb) + nn(g2l, kb)) * use
    out_ref[1] = gather_blocks(tn(g2h, qb) + tn(g2l, qb)) * use


def pinv_back(idx, gmix, lv, k2, save, marks, lm):
    d = lv.shape[1]
    n = marks.shape[0]
    last = d // QUAD - 1
    col = lambda i, s: (0, jnp.minimum(s[1], last))
    col3 = lambda i, s: (0, 0, jnp.minimum(s[1], last))
    cost = pl.CostEstimate(flops=48 * 2 * QUAD**3, bytes_accessed=4 * 10**6, transcendentals=0)
    return pl.pallas_call(
        functools.partial(pinv_back_kernel, lm=lm),
        grid_spec=pltpu.PrefetchScalarGridSpec(
            num_scalar_prefetch=1,
            grid=(1,),
            in_specs=[
                pl.BlockSpec((n, M, QUAD), col3),
                pl.BlockSpec((M, QUAD), col),
                pl.BlockSpec((M, QUAD), col),
                whole(save.shape),
                pl.BlockSpec((n, marks.shape[1], QUAD), col3),
            ],
            out_specs=whole((2, M, QUAD)),
        ),
        out_shape=sds((2, M, QUAD), F32),
        compiler_params=params(),
        cost_estimate=cost,
        name="pinv_back",
    )(idx, gmix, lv, k2, save, marks)


def second_kernel(
    idx, k_ref, v_ref, vedge_ref, gc_ref, gedge_ref, e_ref, gm_ref, gt_ref, marks_ref, doc_ref,
    pad_ref, taps_ref, gk_ref, gv_ref, qm_ref, gtap_ref, vext, gext, band, *, tok,
):
    quad = pl.program_id(0)
    n = marks_ref.shape[0]
    lm = tok // M
    heads = QUAD // M
    half = taps_ref.shape[2] // 2
    mask = block_mask()
    qm = spread_blocks(
        jnp.concatenate([marks_ref[i, 0:lm, :] for i in range(n)], axis=0), mask
    )
    gm = spread_blocks(gm_ref[...], mask)
    lane = iota((M, 128), 1)
    cols = []
    for h in range(heads):
        pick = jnp.where(lane == quad * heads + h, gt_ref[...], 0.0)
        cols.append(jnp.sum(pick, axis=1, keepdims=True))
    gt = jnp.concatenate(cols, axis=0)
    e = e_ref[...]
    g3 = (e.astype(F32) * (nt(gm, v_ref[...]) + gt)).astype(BF)
    qm_ref[...] = gather_blocks(nn(g3, k_ref[...])) * 0.125
    gk_ref[...] = (tn(g3, qm) * 0.125).astype(BF)
    gv = tn(e, gm)
    fill_halo(vext, v_ref, vedge_ref, tok)
    fill_halo(gext, gc_ref, gedge_ref, tok)
    fill_bands(taps_ref.at[0], band, half, True)
    bounds = doc_bounds(doc_ref, idx)
    start = idx[1] * tok
    keep_n = valid_count(pad_ref, idx) - start
    col64 = iota((128, 128), 1)
    pairs = [jnp.zeros((128, 256), F32) for _ in range(heads)]
    for sub in range(tok // 128):
        place = start + sub * 128
        same = (
            docs_at(place + iota((128, 1), 0), bounds, LEN)
            == docs_at(place - 64 + iota((1, 256), 1), bounds, LEN)
        )
        low = same.astype(BF)
        keep = iota((128, 1), 0) < keep_n - sub * 128
        at = slice(sub * 128, sub * 128 + 128)
        for pair in range(heads // 2):
            lanes = slice(pair * 128, pair * 128 + 128)
            back = banded(band, gext[sub * 128 : sub * 128 + 256, lanes], low, 2 * pair)
            gv_ref[at, lanes] = jnp.where(keep, gv[at, lanes] + back, 0.0).astype(BF)
            g = gc_ref[at, lanes]
            win = vext[sub * 128 : sub * 128 + 256, lanes]
            for h in range(2):
                own = jnp.where((col64 < 64) == (h == 0), g, jnp.zeros((), BF))
                pairs[2 * pair + h] += jnp.where(same, nt(own, win), 0.0)
    gap = iota((128, 256), 1) - iota((128, 256), 0) - 64 + half
    out = jnp.zeros((8, 128), F32)
    line, lane8 = iota((8, 128), 0), iota((8, 128), 1)
    for h in range(heads):
        for o in range(2 * half + 1):
            val = jnp.sum(jnp.where(gap == o, pairs[h], 0.0))
            out = jnp.where((line == h) & (lane8 == o), val, out)
    gtap_ref[0] = out


def second_back(idx, k, v, vedge, gc, gedge, e, gm, gt, marks, documents, padding, taps):
    tok, d = k.shape
    n = marks.shape[0]
    heads = QUAD // M
    lane = lambda i, s: (0, i)
    taps3 = taps.reshape(d // QUAD, heads, taps.shape[1])
    cost = pl.CostEstimate(flops=16 * tok * d * QUAD, bytes_accessed=12 * tok * d, transcendentals=0)
    return pl.pallas_call(
        functools.partial(second_kernel, tok=tok),
        grid_spec=pltpu.PrefetchScalarGridSpec(
            num_scalar_prefetch=1,
            grid=(d // QUAD,),
            in_specs=[
                pl.BlockSpec((tok, QUAD), lane),
                pl.BlockSpec((tok, QUAD), lane),
                pl.BlockSpec((32, QUAD), lane),
                pl.BlockSpec((tok, QUAD), lane),
                pl.BlockSpec((32, QUAD), lane),
                pl.BlockSpec((QUAD, tok), lambda i, s: (i, 0)),
                pl.BlockSpec((M, QUAD), lane),
                whole(gt.shape),
                pl.BlockSpec((n, marks.shape[1], QUAD), lambda i, s: (0, 0, i)),
                whole(documents.shape),
                whole(padding.shape),
                pl.BlockSpec((1, heads, taps.shape[1]), lambda i, s: (i, 0, 0)),
            ],
            out_specs=[
                pl.BlockSpec((tok, QUAD), lane),
                pl.BlockSpec((tok, QUAD), lane),
                pl.BlockSpec((M, QUAD), lane),
                pl.BlockSpec((1, 8, 128), lambda i, s: (i, 0, 0)),
            ],
            scratch_shapes=[
                pltpu.VMEM((tok + 128, QUAD), BF),
                pltpu.VMEM((tok + 128, QUAD), BF),
                pltpu.VMEM((heads, 128, 256), BF),
            ],
        ),
        out_shape=[
            sds((tok, d), BF),
            sds((tok, d), BF),
            sds((M, d), F32),
            sds((d // QUAD, 8, 128), F32),
        ],
        compiler_params=params(),
        cost_estimate=cost,
        name="second_back",
    )(idx, k, v, vedge, gc, gedge, e, gm, gt, marks, documents, padding, taps3)


def spread_kernel(idx, gq_ref, gk_ref, got_ref, pad_ref, dq0, dq1, dk0, dk1, *, tok):
    n = got_ref.shape[0]
    lm = tok // M
    d = gq_ref.shape[1]
    half = d // 2
    got = got_ref[0].astype(F32)
    for i in range(1, n):
        got = got + got_ref[i].astype(F32)
    keep_n = valid_count(pad_ref, idx) - idx[1] * tok
    keep = (iota((tok, 1), 0) < keep_n).astype(F32).reshape(lm, M, 1)
    share = keep / jnp.maximum(jnp.sum(keep, axis=1, keepdims=True), 1.0)
    for at, src, outs in ((0, gq_ref, (dq0, dq1)), (lm, gk_ref, (dk0, dk1))):
        mark = got[at : at + lm].reshape(lm, 1, d)
        val = src[...].astype(F32).reshape(lm, M, d) + mark * share
        val = val.reshape(tok, d).astype(BF)
        outs[0][...] = val[:, :half]
        outs[1][...] = val[:, half:]


def spread(idx, gq, gk, got, padding):
    tok, d = gq.shape
    return pl.pallas_call(
        functools.partial(spread_kernel, tok=tok),
        grid_spec=pltpu.PrefetchScalarGridSpec(
            num_scalar_prefetch=1,
            grid=(1,),
            in_specs=[whole(gq.shape), whole(gk.shape), whole(got.shape), whole(padding.shape)],
            out_specs=[whole((tok, d // 2))] * 4,
        ),
        out_shape=[sds((tok, d // 2), BF)] * 4,
        compiler_params=params(),
        name="spread",
    )(idx, gq, gk, got, padding)


def inputs_kernel(idx, gh1_ref, dq0, dq1, dk0, dk1, dv_ref, q0, q1, k0, k1, v0, v1, out_ref):
    half = dq0.shape[1]
    acc = gh1_ref[...].astype(F32)
    acc = acc + nt(dq0[...], q0[...]) + nt(dq1[...], q1[...])
    acc = acc + nt(dk0[...], k0[...]) + nt(dk1[...], k1[...])
    acc = acc + nt(dv_ref[:, :half], v0[...]) + nt(dv_ref[:, half:], v1[...])
    out_ref[0] = acc.astype(BF)


def inputs_grad(idx, gh1, dq, dk, dv, wq, wk, wv):
    tok, d = gh1.shape
    half = d // 2
    rows = 512
    tokb = lambda j, i, s: (i, 0)
    wspec = pl.BlockSpec((half, half), lambda j, i, s: (s[0] ^ j, 0))
    cost = pl.CostEstimate(flops=6 * tok * d * d, bytes_accessed=12 * tok * d, transcendentals=0)
    return pl.pallas_call(
        inputs_kernel,
        grid_spec=pltpu.PrefetchScalarGridSpec(
            num_scalar_prefetch=1,
            grid=(2, tok // rows),
            in_specs=[pl.BlockSpec((rows, half), lambda j, i, s: (i, s[0] ^ j))]
            + [pl.BlockSpec((rows, half), tokb)] * 4
            + [pl.BlockSpec((rows, d), tokb)]
            + [wspec] * 6,
            out_specs=pl.BlockSpec((1, rows, half), lambda j, i, s: (j, i, 0)),
        ),
        out_shape=sds((2, tok, half), BF),
        compiler_params=params(),
        cost_estimate=cost,
        name="inputs_grad",
    )(idx, gh1, *dq, *dk, dv, *wq, *wk, *wv)


def shards(
    inputs,
    cotangent,
    padding,
    documents,
    w_query,
    w_key,
    w_value,
    w_out,
    w_up,
    w_down,
    conv_taps,
    gain_attn,
    shift_attn,
    gain_ffn,
    shift_ffn,
):
    row_count, tok, d = inputs.shape
    seq_n, dp_n = lax.axis_size("seq"), lax.axis_size("dp")
    mp, seq, dp = lax.axis_index("mp"), lax.axis_index("seq"), lax.axis_index("dp")
    lm = tok // M
    chunk = d // (seq_n * dp_n)
    fast = seq_n == 4 and dp_n == 4 and chunk % 16 == 0
    shape = (dp_n if fast else 0, seq_n, chunk)
    idx = jnp.stack(
        [mp, seq, dp, jnp.full((), min(d // QUAD, seq_n), jnp.int32)]
    ).astype(jnp.int32)

    def swap(a):
        return lax.ppermute(a, "mp", [(0, 1), (1, 0)])

    wq, wk, wv = ((w, swap(w)) for w in (w_query, w_key, w_value))
    wo, wu, wd = ((w, swap(w)) for w in (w_out, w_up, w_down))
    taps = jnp.concatenate([conv_taps, swap(conv_taps)], axis=0)
    q, k, v, pack = project(idx, inputs, padding, (*wq, *wk, *wv), tok)
    marks, vedge = gather_seq(seq_n, [pack[: 2 * lm]], pack[2 * lm :], 1)
    k1, e, mix, stat = scores(idx, q, k, v, marks, padding)
    k2, inv, save = pinv(idx, marks, lm)
    mixes, stats = gather_seq(seq_n, [mix, stat], None, 2)
    cm, lv, gst = combine(idx, mixes, stats, inv)
    vecs = [a.reshape(1, d) for a in (gain_attn, shift_attn, gain_ffn, shift_ffn)]
    out_own, ctx, h1, nl, act0, act1, gp0, gp1, gh2, acc_f = forward(
        idx, inputs, cotangent, padding, documents, v, vedge, k1, cm, taps, wo, wu, wd, vecs
    )
    out_other = swap(out_own)
    g_down = weight_grads(idx, [(gh2, 0)], [[act0, act1]], 256, shape)
    down_other = swap(g_down[1])
    du0, du1, gh1, gc, acc_b = backward(idx, gh2, h1, (gp0, gp1), wo, wu, wd, vecs[0])
    g_up = weight_grads(idx, [(nl, 0)], [[du0, du1]], 256, shape)
    up_other = swap(g_up[1])
    half = d // 2
    g_out = weight_grads(idx, [(gh1, 0)], [[ctx[:, :half], ctx[:, half:]]], 128, shape)
    out_w_other = swap(g_out[1])
    gq, gmix, gkm = first_back(q, k1, gc, cm, marks)
    gedge_own = jnp.concatenate([gc[:16], gc[tok - 16 :]], axis=0)
    gmixes, gedge = gather_seq(seq_n, [gmix], gedge_own, 3)
    gm, gt = middle(idx, gmixes, lv, inv, gst)
    two = pinv_back(idx, gmixes, lv, k2, save, marks, lm)
    gk, gv, gqm, gtap = second_back(
        idx, k, v, vedge, gc, gedge, e, gm, gt, marks, documents, padding, taps
    )
    at = jnp.minimum(seq, d // QUAD - 1) * QUAD
    gqm = gqm + lax.dynamic_update_slice(jnp.zeros((M, d), F32), two[0], (0, at))
    gkm = gkm + lax.dynamic_update_slice(jnp.zeros((M, d), F32), two[1], (0, at))
    both = jnp.concatenate(
        [gqm.reshape(seq_n, lm, d), gkm.reshape(seq_n, lm, d)], axis=1
    ).astype(BF)
    got = scatter_seq(seq_n, both, 4)
    dq0, dq1, dk0, dk1 = spread(idx, gq, gk, got, padding)
    dq1_got, dk1_got, dv1_got = swap(dq1), swap(dk1), swap(gv[:, half:])
    g_qkv = weight_grads(
        idx,
        [(inputs, 0), (inputs, 1)],
        [[dq0, dk0, gv[:, :half]], [dq1_got, dk1_got, dv1_got]],
        128,
        shape,
    )
    gin = inputs_grad(idx, gh1, (dq0, dq1), (dk0, dk1), gv, wq, wk, wv)
    gin_other = swap(gin[1])

    reduce = reduce_fast if fast else reduce_any

    def add(a, b):
        return (a.astype(F32) + b.astype(F32)).astype(BF)

    sum_down = reduce(add(g_down[0], down_other))
    sum_up = reduce(add(g_up[0], up_other))
    sum_out = reduce(add(g_out[0], out_w_other))
    sum_qkv = reduce(jnp.concatenate(g_qkv, axis=1))

    def rows_of(own, other):
        return jnp.where(mp == 0, jnp.stack([own, other]), jnp.stack([other, own]))

    heads = conv_taps.shape[0]
    tap_all = gtap[:, : QUAD // M, : conv_taps.shape[1]].reshape(2, heads, -1)
    tap_all = jnp.where(mp == 0, tap_all, tap_all[::-1])
    squares = jnp.sum(acc_f[2:5], axis=1)
    place = jnp.arange(dp_n * row_count, dtype=jnp.int32) == dp * row_count + mp
    squares = jnp.where(place[:, None], squares[None, :], 0.0)
    tap_all, norms, squares = lax.psum(
        (tap_all, jnp.concatenate([acc_b[:2], acc_f[:2]], axis=0), squares), ("dp", "seq", "mp")
    )
    tap_total = lax.dynamic_index_in_dim(tap_all, mp, 0, keepdims=False)
    own_squares = lax.dynamic_slice_in_dim(squares, dp * row_count, row_count, 0)
    row_valid = jnp.sum(padding.astype(F32), axis=1)
    row_rms = jnp.sqrt(own_squares / (row_valid[:, None] * d) + 1e-06)
    return (
        rows_of(out_own, out_other),
        rows_of(gin[0], gin_other),
        sum_qkv[:, :half],
        sum_qkv[:, half : 2 * half],
        sum_qkv[:, 2 * half :],
        sum_out.T,
        sum_up,
        sum_down.T,
        tap_total,
        norms[0],
        norms[1],
        norms[2],
        norms[3],
        row_rms,
    )


def solution(mesh):
    return jax.shard_map(
        shards,
        mesh=mesh,
        in_specs=(
            P("dp", "seq", None),
            P("dp", "seq", None),
            P("dp", None),
            P("dp", None),
            P(None, "mp"),
            P(None, "mp"),
            P(None, "mp"),
            P("mp", None),
            P(None, "mp"),
            P("mp", None),
            P("mp", None),
            P(),
            P(),
            P(),
            P(),
        ),
        out_specs=(
            P("dp", "seq", None),
            P("dp", "seq", "mp"),
            P(("dp", "seq"), "mp"),
            P(("dp", "seq"), "mp"),
            P(("dp", "seq"), "mp"),
            P("mp", ("dp", "seq")),
            P(("dp", "seq"), "mp"),
            P("mp", ("dp", "seq")),
            P("mp", None),
            P(),
            P(),
            P(),
            P(),
            P("dp", None),
        ),
        check_vma=False,
    )
```

time: 1060 us -> 453 us (0.43)
  waiting for transfers between devices: 355 us -> 83.6 us
  Pallas kernels: 0 us -> 238 us
  matrix products: 233 us -> 0 us
  other arithmetic: 158 us -> 18.1 us
  local copies, waits for them, and re-layouts: 150 us -> 28.5 us
  blocking collectives: 125 us -> 40.5 us
  starting transfers between devices: 12 us -> 38.2 us
  between operations: 19.5 us -> 1.52 us
    reduce_scatter x8 -> x0, waiting for transfers between devices: 257 us -> none  [the longest x1 85 us: shards(): lax.psum_scatter(weight_terms[5], 'dp', scatter_dimension=1, tiled=True)]
    pallas_call x0 -> x20, Pallas kernels: none -> 238 us  [the longest x4 43 us: weight_grads(): pl.pallas_call(functools.partial(weight_kernel, nl=nl, nr=nr, blocks=bloc...]
    dot_general x110 -> x0, matrix products: 233 us -> none  [the longest x6 40.3 us: right_product(): lax.dot_general(left, right, (((1,), (1,)), ((), ())), preferred_element_...]
    psum x5 -> x0, waiting for transfers between devices: 96.9 us -> none  [the longest x1 33.1 us: shards(): lax.psum(jnp.dot(act_low, w_down, preferred_element_type=jnp.float32), 'mp')]
    ppermute x4 -> x43, waiting for transfers between devices: 0.01 us -> 83.6 us  [the longest x4 35.7 us: reduce_fast(): got_a = lax.ppermute(send_a, 'seq', halving(seq_n, 1))]
    convert_element_type x14 -> x19, other arithmetic: 80.5 us -> 2.73 us  [the longest x3 1.38 us: add(): return (a.astype(F32) + b.astype(F32)).astype(BF)]
    psum x3 -> x1, blocking collectives: 94 us -> 40.5 us  [shards(): lax.psum((tap_all, jnp.concatenate([acc_b[:2], acc_f[:2]], axis=0), squar...]
    reduce_sum x17 -> x2, other arithmetic: 44.2 us -> 1.76 us  [the longest x1 0.9 us: shards(): row_valid = jnp.sum(padding.astype(F32), axis=1)]
  transfers between devices with their start and end apart: 22 -> 43, of which waited for: 10 -> 15; matrix products, arithmetic and copies ran while one was open for 26% -> 7% of each run, Pallas kernels for 0% -> 26%
where the time goes in v1:
time: 453 us; the launch traced here: 449 us
  Pallas kernels  238 us (53%)
  waiting for transfers between devices  83.6 us (18%)
  blocking collectives  40.5 us (9%)
  starting transfers between devices  38.2 us (8%)
  local copies, waits for them, and re-layouts  28.5 us (6%)
  other arithmetic  18.1 us (4%)
    pallas_call x4, Pallas kernels, weight_grads(): pl.pallas_call(functools.partial(weight_kernel, nl=nl, nr=nr, blocks=bloc...  43 us
    psum x1, blocking collectives, shards(): lax.psum((tap_all, jnp.concatenate([acc_b[:2], acc_f[:2]], axis=0), squar...  40.5 us
    pallas_call x1, Pallas kernels, forward(): pl.pallas_call(functools.partial(forward_kernel, tok=tok), grid_spec=pltp...  40 us
    ppermute x4, waiting for transfers between devices, reduce_fast(): got_a = lax.ppermute(send_a, 'seq', halving(seq_n, 1))  35.7 us
    ppermute x12, waiting for transfers between devices, reduce_fast(): lax.ppermute(c[p * ch:(p + 1) * ch], 'dp', halving(dp_n, p)).astype(F32)  26.1 us
    pallas_call x3, Pallas kernels, gather_seq(): pl.pallas_call(body, in_specs=[pl.BlockSpec(memory_space=pl.ANY)] * len(a...  25 us
    pallas_call x1, Pallas kernels, pinv(): pl.pallas_call(functools.partial(pinv_kernel, lm=lm), grid_spec=pltpu.Pre...  24.4 us
    pallas_call x1, Pallas kernels, backward(): pl.pallas_call(backward_kernel, grid_spec=pltpu.PrefetchScalarGridSpec(nu...  23 us
  transfers between devices with their start and end apart: 43, of which 15 were waited for; matrix products, arithmetic and copies ran while one was open for 7% of the time, Pallas kernels for 26%

profile of v1, /device:TPU:0, one launch (start us, length us, event | category | flops | bytes accessed | tf_op | source)
XLA Modules:
  0.0 448.6 jit_solution(9652320099167100151)
XLA Ops:
  15.6 9.6 %project.1 = (bf16[1024,768]{1,0:T(8,128)(2,1)}, bf16[1024,768]{1,0:T(8,128)(2,1)}, bf16[1024,768]{1,0:T(8,128)(2,1)}, bf16[64,768]{1,0:T(8,128)(2,1)}) custom-call(s32[4]{0:T(128)} %pad_add_fusion.idx, bf16[2,1024,768]{2,1,0:T(8,128)(2,1)} %refs_1_.1, s32[2,4096]{1,0:T(2,128)} %pad_ref.9, bf16[768,384]{1,0:T(8,128)(2,1)} %q0.3, ...), custom_call_target="tpu_custom_call" | custom-call | flops 3623878656 | bytes 9437184 | tf_op jit(solution)/shard_map/project/pallas_call | solution.py:127
  26.1 8.3 %gather1.1 = (bf16[4,32,768]{2,1,0:T(8,128)(2,1)S(1)}, bf16[32,768]{1,0:T(8,128)(2,1)S(1)}) custom-call(bf16[32,768]{1,0:T(8,128)(2,1)S(1)} %get-tuple-element.179.refs_0_, bf16[32,768]{1,0:T(8,128)(2,1)S(1)} %get-tuple-element.178.refs_1_), custom_call_target="tpu_custom_call" | custom-call | tf_op jit(solution)/shard_map/gather1/pallas_call | solution.py:231
  35.8 7.1 %scores.1 = (bf16[768,1024]{1,0:T(8,128)(2,1)}, bf16[768,1024]{1,0:T(8,128)(2,1)}, bf16[64,768]{1,0:T(8,128)(2,1)}, f32[64,128]{1,0:T(8,128)}) custom-call(s32[4]{0:T(128)} %pad_add_fusion.idx, bf16[1024,768]{1,0:T(8,128)(2,1)} %get-tuple-element.74.q_ref, bf16[1024,768]{1,0:T(8,128)(2,1)} %get-tuple-element.75.k_ref, ...), custom_call_target="tpu_custom_call" | custom-call | flops 1207959552 | bytes 7864320 | tf_op jit(solution)/shard_map/scores/pallas_call | solution.py:321
  44.5 8.6 %gather2.1 = (bf16[4,64,768]{2,1,0:T(8,128)(2,1)S(1)}, f32[4,64,128]{2,1,0:T(8,128)S(1)}) custom-call(bf16[64,768]{1,0:T(8,128)(2,1)S(1)} %copy-done.6, f32[64,128]{1,0:T(8,128)S(1)} %copy-done.7), custom_call_target="tpu_custom_call" | custom-call | tf_op jit(solution)/shard_map/gather2/pallas_call | solution.py:231
  54.5 24.4 %pinv.1 = (f32[64,768]{1,0:T(8,128)}, f32[64,768]{1,0:T(8,128)}, bf16[6,4,256,256]{3,2,1,0:T(8,128)(2,1)}) custom-call(s32[4]{0:T(128)} %pad_add_fusion.idx, bf16[4,32,768]{2,1,0:T(8,128)(2,1)} %copy-done.3), custom_call_target="tpu_custom_call" | custom-call | flops 7247757312 | bytes 4000000 | tf_op jit(solution)/shard_map/pinv/pallas_call | solution.py:399
  78.8 3.7 combine.1
  83.4 40.0 %forward.1 = (bf16[1024,768]{1,0:T(8,128)(2,1)}, bf16[1024,768]{1,0:T(8,128)(2,1)}, f32[1024,768]{1,0:T(8,128)}, bf16[1024,768]{1,0:T(8,128)(2,1)}, bf16[1024,15...) custom-call(s32[4]{0:T(128)} %pad_add_fusion.idx, ...), custom_call_target="tpu_custom_call" | custom-call | flops 9663676416 | bytes 47185920 | tf_op jit(solution)/shard_map/forward/pallas_call | solution.py:651
  125.0 23.0 %backward.1 = (bf16[1024,1536]{1,0:T(8,128)(2,1)}, bf16[1024,1536]{1,0:T(8,128)(2,1)}, bf16[1024,768]{1,0:T(8,128)(2,1)}, bf16[1024,768]{1,0:T(8,128)(2,1)}, f32[8,768]{1,0:T(8,128)}) custom-call(s32[4]{0:T(128)} %pad_add_fusion.idx, f32[1024,768]{1,0:T(8,128)} %get-tuple-element.85.gh2_ref.refs_0_, f32[1024,768]{1,0:T(8,128)} %get-tuple-element.86.h1_ref, ...), custom_call_target="tpu_custom_call" | custom-call | flops 9663676416 | bytes 31457280 | tf_op jit(solution)/shard_map/backward/pallas_call | solution.py:721
  148.0 5.4 %first_back.1 = (bf16[1024,768]{1,0:T(8,128)(2,1)}, bf16[64,768]{1,0:T(8,128)(2,1)}, f32[64,768]{1,0:T(8,128)}) custom-call(bf16[1024,768]{1,0:T(8,128)(2,1)} %get-tuple-element.74.q_ref, bf16[768,1024]{1,0:T(8,128)(2,1)} %get-tuple-element.77.k1_ref, bf16[1024,768]{1,0:T(8,128)(2,1)} %get-tuple-element.90.gc_ref, bf16[64,768]{1,0:T(8,128)(2,1)} %get-tuple-element.83.cm_ref, ...), custom_call_target="tpu_custom_call" | custom-call | flops 1610612736 | bytes 6291456 | tf_op jit(solution)/shard_map/first_back/pallas_call | solution.py:870
  155.8 8.0 %gather3.1 = (bf16[4,64,768]{2,1,0:T(8,128)(2,1)S(1)}, bf16[32,768]{1,0:T(8,128)(2,1)S(1)}) custom-call(bf16[64,768]{1,0:T(8,128)(2,1)S(1)} %copy-done.5, bf16[32,768]{1,0:T(8,128)(2,1)S(1)} %pad_maximum_fusion.8.refs_1_), custom_call_target="tpu_custom_call" | custom-call | tf_op jit(solution)/shard_map/gather3/pallas_call | solution.py:231
  165.2 4.3 middle.1
  169.5 22.0 %second_back.1 = (bf16[1024,768]{1,0:T(8,128)(2,1)}, bf16[1024,768]{1,0:T(8,128)(2,1)}, f32[64,768]{1,0:T(8,128)}, f32[3,8,128]{2,1,0:T(8,128)}) custom-call(s32[4]{0:T(128)} %pad_add_fusion.idx, bf16[1024,768]{1,0:T(8,128)(2,1)} %get-tuple-element.75.k_ref, bf16[1024,768]{1,0:T(8,128)(2,1)} %get-tuple-element.71.v_ref, bf16[32,768]{1,0:T(8,128)(2,1)} %copy-done.8, ...), custom_call_target="tpu_custom_call" | custom-call | flops 3221225472 | bytes 9437184 | tf_op jit(solution)/shard_map/second_back/pallas_call | solution.py:1081
  192.2 8.8 %pinv_back.1 = f32[2,64,256]{2,1,0:T(8,128)} custom-call(s32[4]{0:T(128)} %pad_add_fusion.idx, bf16[4,64,768]{2,1,0:T(8,128)(2,1)} %copy-done.1, f32[64,768]{1,0:T(8,128)} %get-tuple-element.96.lv_ref, f32[64,768]{1,0:T(8,128)} %get-tuple-element.102.k2_ref, bf16[6,4,256,256]{3,2,1,0:T(8,128)(2,1)} %get-tuple-element.103.save_ref, bf16[4,32,768]{2,1,0:T(8,128)(2,1)} %copy-done.3), custom_call_target="tpu_custom_call" | custom-call | flops 1610612736 | bytes 4000000 | tf_op jit(solution)/shard_map/pinv_back/pallas_call | solution.py:992
  202.1 5.4 %scatter4.1.got_ref = bf16[4,32,768]{2,1,0:T(8,128)(2,1)S(1)} custom-call(bf16[4,32,768]{2,1,0:T(8,128)(2,1)S(1)} %pad_maximum_fusion.3.src), custom_call_target="tpu_custom_call" | custom-call | tf_op jit(solution)/shard_map/scatter4/pallas_call | solution.py:270
  209.2 5.4 %spread.1 = (bf16[1024,384]{1,0:T(8,128)(2,1)}, bf16[1024,384]{1,0:T(8,128)(2,1)}, bf16[1024,384]{1,0:T(8,128)(2,1)}, bf16[1024,384]{1,0:T(8,128)(2,1)}) custom-call(s32[4]{0:T(128)} %pad_add_fusion.idx, bf16[1024,768]{1,0:T(8,128)(2,1)} %get-tuple-element.91.gq_ref, bf16[1024,768]{1,0:T(8,128)(2,1)} %get-tuple-element.100.gk_ref, ...), custom_call_target="tpu_custom_call" | custom-call | tf_op jit(solution)/shard_map/spread/pallas_call | solution.py:1145
  215.2 11.0 %inputs_grad.1 = bf16[2,1024,384]{2,1,0:T(8,128)(2,1)} custom-call(s32[4]{0:T(128)} %pad_add_fusion.idx, bf16[1024,768]{1,0:T(8,128)(2,1)} %get-tuple-element.89.gh1_ref.refs_0_, bf16[1024,384]{1,0:T(8,128)(2,1)} %get-tuple-element.105.dq0.refs_2_, bf16[1024,384]{1,0:T(8,128)(2,1)} %get-tuple-element.106.dq1, ...), custom_call_target="tpu_custom_call" | custom-call | flops 3623878656 | bytes 9437184 | tf_op jit(solution)/shard_map/inputs_grad/pallas_call | solution.py:1175
  230.6 6.9 %weights.5 = (bf16[768,384]{1,0:T(8,128)(2,1)}, bf16[768,384]{1,0:T(8,128)(2,1)}) custom-call(s32[4]{0:T(128)} %pad_add_fusion.idx, bf16[1024,768]{1,0:T(8,128)(2,1)} %get-tuple-element.89.gh1_ref.refs_0_, bf16[1024,384]{1,0:T(8,128)(2,1)} %get-tuple-element.144.refs_1_, bf16[1024,384]{1,0:T(8,128)(2,1)} %get-tuple-element.143.refs_2_), custom_call_target="tpu_custom_call" | custom-call | flops 1207959552 | bytes 3145728 | tf_op jit(solution)/shard_map/weights/pallas_call | solution.py:799
  237.4 11.7 %weights.7 = (bf16[768,1536]{1,0:T(8,128)(2,1)}, bf16[768,1536]{1,0:T(8,128)(2,1)}) custom-call(s32[4]{0:T(128)} %pad_add_fusion.idx, f32[1024,768]{1,0:T(8,128)} %get-tuple-element.85.gh2_ref.refs_0_, bf16[1024,1536]{1,0:T(8,128)(2,1)} %get-tuple-element.121.refs_1_, bf16[1024,1536]{1,0:T(8,128)(2,1)} %get-tuple-element.122.refs_2_), custom_call_target="tpu_custom_call" | custom-call | flops 4831838208 | bytes 12582912 | tf_op jit(solution)/shard_map/weights/pallas_call | solution.py:799
  249.2 40.5 %all-reduce = (f32[2,6,33]{2,1,0:T(8,128)S(1)}, f32[4,768]{1,0:T(4,128)S(1)}, f32[8,3]{1,0:T(8,128)S(1)}) all-reduce(f32[2,6,33]{2,1,0:T(8,128)S(1)} %reverse_select_fusion, f32[4,768]{1,0:T(4,128)S(1)} %pad_maximum_fusion.10, f32[8,3]{1,0:T(8,128)S(1)} %broadcast_select_fusion), channel_id=1, replica_groups=mesh['dp'=4,'seq'=4,'mp'=2] {'dp','seq','mp'}, use_global_device_ids=true, to_apply=%region_0.1 | all-reduce | flops 3492 | bytes 27936 | tf_op jit(solution)/shard_map/psum | solution.py:1292
  291.6 11.4 %weights.6 = (bf16[768,1536]{1,0:T(8,128)(2,1)}, bf16[768,1536]{1,0:T(8,128)(2,1)}) custom-call(s32[4]{0:T(128)} %pad_add_fusion.idx, bf16[1024,768]{1,0:T(8,128)(2,1)} %get-tuple-element.116.refs_0_, bf16[1024,1536]{1,0:T(8,128)(2,1)} %get-tuple-element.117.refs_1_, bf16[1024,1536]{1,0:T(8,128)(2,1)} %get-tuple-element.118.refs_2_), custom_call_target="tpu_custom_call" | custom-call | flops 4831838208 | bytes 12582912 | tf_op jit(solution)/shard_map/weights/pallas_call | solution.py:799
  311.3 3.6 collective-permute-done.22
  318.3 13.1 %weights.4 = (bf16[768,384]{1,0:T(8,128)(2,1)}, bf16[768,384]{1,0:T(8,128)(2,1)}, bf16[768,384]{1,0:T(8,128)(2,1)}) custom-call(s32[4]{0:T(128)} %pad_add_fusion.idx, bf16[2,1024,768]{2,1,0:T(8,128)(2,1)} %refs_1_.1, bf16[2,1024,768]{2,1,0:T(8,128)(2,1)} %refs_1_.1, bf16[1024,384]{1,0:T(8,128)(2,1)} %get-tuple-element.105.dq0.refs_2_, ...), custom_call_target="tpu_custom_call" | custom-call | flops 3623878656 | bytes 3145728 | tf_op jit(solution)/shard_map/weights/pallas_call | solution.py:799
  335.1 11.1 %collective-permute-done.12 = bf16[384,576]{1,0:T(8,128)(2,1)S(1)} collective-permute-done((bf16[384,576]{1,0:T(8,128)(2,1)S(1)}, bf16[384,576]{1,0:T(8,128)(2,1)S(1)}, u32[]{:S(2)}, u32[]{:S(2)}) %collective-permute-start.12) | collective-permute-done | bytes 442400 | tf_op jit(solution)/shard_map/ppermute | solution.py:828
  349.4 4.8 %collective-permute-done.13 = bf16[192,576]{1,0:T(8,128)(2,1)S(1)} collective-permute-done((bf16[192,576]{1,0:T(8,128)(2,1)S(1)}, bf16[192,576]{1,0:T(8,128)(2,1)S(1)}, u32[]{:S(2)}, u32[]{:S(2)}) %collective-permute-start.13) | collective-permute-done | bytes 221216 | tf_op jit(solution)/shard_map/ppermute | solution.py:832
  355.6 4.9 %collective-permute-done.15 = bf16[192,576]{1,0:T(8,128)(2,1)S(1)} collective-permute-done((bf16[192,576]{1,0:T(8,128)(2,1)S(1)}, bf16[192,576]{1,0:T(8,128)(2,1)S(1)}, u32[]{:S(2)}, u32[]{:S(2)}) %collective-permute-start.15) | collective-permute-done | bytes 221216 | tf_op jit(solution)/shard_map/ppermute | solution.py:833
  376.1 4.6 %collective-permute-done.17 = bf16[48,1152]{1,0:T(8,128)(2,1)S(1)} collective-permute-done((bf16[48,1152]{1,0:T(8,128)(2,1)S(1)}, bf16[48,1152]{1,0:T(8,128)(2,1)S(1)}, u32[]{:S(2)}, u32[]{:S(2)}) %collective-permute-start.17) | collective-permute-done | bytes 110624 | tf_op jit(solution)/shard_map/ppermute | solution.py:838
  381.5 4.9 %maximum_select_fusion = bf16[2,1024,768]{2,1,0:T(8,128)(2,1)} fusion(bf16[1,1024,768]{2,1,0:T(8,128)(2,1)} %bitcast.4, bf16[1,1024,768]{2,1,0:T(8,128)(2,1)} %bitcast.3, pred[]{:T(512)S(6)} %eq.15), kind=kLoop, calls=%fused_computation.2 | loop fusion | flops 4718592 | bytes 6291457 | tf_op jit(solution)/shard_map/jit(_where)/select_n | solution.py:1284
  392.3 11.1 %collective-permute-done.28 = bf16[384,768]{1,0:T(8,128)(2,1)S(1)} collective-permute-done((bf16[384,768]{1,0:T(8,128)(2,1)S(1)}, bf16[384,768]{1,0:T(8,128)(2,1)S(1)}, u32[]{:S(2)}, u32[]{:S(2)}) %collective-permute-start.28) | collective-permute-done | bytes 589856 | tf_op jit(solution)/shard_map/ppermute | solution.py:828
  405.9 10.1 %collective-permute-done.36 = bf16[384,768]{1,0:T(8,128)(2,1)S(1)} collective-permute-done((bf16[384,768]{1,0:T(8,128)(2,1)S(1)}, bf16[384,768]{1,0:T(8,128)(2,1)S(1)}, u32[]{:S(2)}, u32[]{:S(2)}) %collective-permute-start.36) | collective-permute-done | bytes 589856 | tf_op jit(solution)/shard_map/ppermute | solution.py:828
  418.6 5.1 %collective-permute-done.29 = bf16[192,768]{1,0:T(8,128)(2,1)S(1)} collective-permute-done((bf16[192,768]{1,0:T(8,128)(2,1)S(1)}, bf16[192,768]{1,0:T(8,128)(2,1)S(1)}, u32[]{:S(2)}, u32[]{:S(2)}) %collective-permute-start.29) | collective-permute-done | bytes 294944 | tf_op jit(solution)/shard_map/ppermute | solution.py:832
  431.0 4.0 collective-permute-done.32
  435.3 9.1 %collective-permute-done.33 = bf16[48,1536]{1,0:T(8,128)(2,1)S(1)} collective-permute-done((bf16[48,1536]{1,0:T(8,128)(2,1)S(1)}, bf16[48,1536]{1,0:T(8,128)(2,1)S(1)}, u32[]{:S(2)}, u32[]{:S(2)}) %collective-permute-start.33) | collective-permute-done | bytes 147488 | tf_op jit(solution)/shard_map/ppermute | solution.py:838
  (209 shorter events, 95.1 us)
Async XLA Ops:
  0.6 81.9 %collective-permute-start.5 = (bf16[768,1536]{1,0:T(8,128)(2,1)}, bf16[768,1536]{1,0:T(8,128)(2,1)}, u32[]{:S(2)}, u32[]{:S(2)}) collective-permute-start(bf16[768,1536]{1,0:T(8,128)(2,1)} %wu0.3), channel_id=1, source_target_pairs={{0,1},{1,0},{2,3},{3,2},{4,5},{5,4},{6,7},{7,6},{8,9},{9,8},{10,11... | collective-permute-start | bytes 7077896 | tf_op jit(solution)/shard_map/ppermute | solution.py:1222
  1.2 81.4 %collective-permute-start.6 = (bf16[1536,768]{1,0:T(8,128)(2,1)}, bf16[1536,768]{1,0:T(8,128)(2,1)}, u32[]{:S(2)}, u32[]{:S(2)}) collective-permute-start(bf16[1536,768]{1,0:T(8,128)(2,1)} %wd0.3), channel_id=1, source_target_pairs={{0,1},{1,0},{2,3},{3,2},{4,5},{5,4},{6,7},{7,6},{8,9},{9,8},{10,11... | collective-permute-start | bytes 7077896 | tf_op jit(solution)/shard_map/ppermute | solution.py:1222
  1.7 12.1 %collective-permute-start = (bf16[768,384]{1,0:T(8,128)(2,1)}, bf16[768,384]{1,0:T(8,128)(2,1)S(1)}, u32[]{:S(2)}, u32[]{:S(2)}) collective-permute-start(bf16[768,384]{1,0:T(8,128)(2,1)} %q0.3), channel_id=1, source_target_pairs={{0,1},{1,0},{2,3},{3,2},{4,5},{5,4},{6,7},{7,6},{8,9},{9,8},{10,11... | collective-permute-start | bytes 1769480 | tf_op jit(solution)/shard_map/ppermute | solution.py:1222
  1.8 12.2 %collective-permute-start.1 = (bf16[768,384]{1,0:T(8,128)(2,1)}, bf16[768,384]{1,0:T(8,128)(2,1)S(1)}, u32[]{:S(2)}, u32[]{:S(2)}) collective-permute-start(bf16[768,384]{1,0:T(8,128)(2,1)} %k0.3), channel_id=1, source_target_pairs={{0,1},{1,0},{2,3},{3,2},{4,5},{5,4},{6,7},{7,6},{8,9},{9,8},{10,11... | collective-permute-start | bytes 1769480 | tf_op jit(solution)/shard_map/ppermute | solution.py:1222
  13.8 68.7 %collective-permute-start.4 = (bf16[384,768]{1,0:T(8,128)(2,1)}, bf16[384,768]{1,0:T(8,128)(2,1)S(1)}, u32[]{:S(2)}, u32[]{:S(2)}) collective-permute-start(bf16[384,768]{1,0:T(8,128)(2,1)} %wo0.3), channel_id=1, source_target_pairs={{0,1},{1,0},{2,3},{3,2},{4,5},{5,4},{6,7},{7,6},{8,9},{9,8},{10,11... | collective-permute-start | bytes 1769480 | tf_op jit(solution)/shard_map/ppermute | solution.py:1222
  214.7 100.8 %collective-permute-start.9 = (bf16[1024,384]{1,0:T(8,128)(2,1)}, bf16[1024,384]{1,0:T(8,128)(2,1)}, u32[]{:S(2)}, u32[]{:S(2)}) collective-permute-start(bf16[1024,384]{1,0:T(8,128)(2,1)} %get-tuple-element.106.dq1), channel_id=1, source_target_pairs={{0,1},{1,0},{2,3},{3,2},{4,5},{5,4},{6,7},{7,6},{8,9},{9,8},{10,11... | collective-permute-start | bytes 2359304 | tf_op jit(solution)/shard_map/ppermute | solution.py:1222
  214.7 102.9 %collective-permute-start.10 = (bf16[1024,384]{1,0:T(8,128)(2,1)}, bf16[1024,384]{1,0:T(8,128)(2,1)}, u32[]{:S(2)}, u32[]{:S(2)}) collective-permute-start(bf16[1024,384]{1,0:T(8,128)(2,1)} %get-tuple-element.108.dk1), channel_id=1, source_target_pairs={{0,1},{1,0},{2,3},{3,2},{4,5},{5,4},{6,7},{7,6},{8,9},{9,8},{10,11... | collective-permute-start | bytes 2359304 | tf_op jit(solution)/shard_map/ppermute | solution.py:1222
  228.8 134.2 %collective-permute-start.8 = (bf16[1024,384]{1,0:T(8,128)(2,1)}, bf16[1024,384]{1,0:T(8,128)(2,1)}, u32[]{:S(2)}, u32[]{:S(2)}) collective-permute-start(bf16[1024,384]{1,0:T(8,128)(2,1)} %get-tuple-element.148), channel_id=1, source_target_pairs={{0,1},{1,0},{2,3},{3,2},{4,5},{5,4},{6,7},{7,6},{8,9},{9,8},{10,11... | collective-permute-start | bytes 2359304 | tf_op jit(solution)/shard_map/ppermute | solution.py:1222
  228.8 86.2 %collective-permute-start.11 = (bf16[1024,384]{1,0:T(8,128)(2,1)S(1)}, bf16[1024,384]{1,0:T(8,128)(2,1)}, u32[]{:S(2)}, u32[]{:S(2)}) collective-permute-start(bf16[1024,384]{1,0:T(8,128)(2,1)S(1)} %get-tuple-element.145), channel_id=1, source_target_pairs={{0,1},{1,0},{2,3},{3,2},{4,5},{5,4},{6,7},{7,6},{8,9},{9,8},{10,11... | collective-permute-start | bytes 2359304 | tf_op jit(solution)/shard_map/ppermute | solution.py:1222
  237.4 65.5 %collective-permute-start.19 = (bf16[768,384]{1,0:T(8,128)(2,1)}, bf16[768,384]{1,0:T(8,128)(2,1)S(1)}, u32[]{:S(2)}, u32[]{:S(2)}) collective-permute-start(bf16[768,384]{1,0:T(8,128)(2,1)} %get-tuple-element.115), channel_id=1, source_target_pairs={{0,1},{1,0},{2,3},{3,2},{4,5},{5,4},{6,7},{7,6},{8,9},{9,8},{10,11... | collective-permute-start | bytes 1769480 | tf_op jit(solution)/shard_map/ppermute | solution.py:1222
  314.8 66.7 %collective-permute-start.7 = (bf16[1024,768]{1,0:T(8,128)(2,1)}, bf16[1024,768]{1,0:T(8,128)(2,1)}, u32[]{:S(2)}, u32[]{:S(2)}) collective-permute-start(bf16[1024,768]{1,0:T(8,128)(2,1)} %get-tuple-element.84), channel_id=1, source_target_pairs={{0,1},{1,0},{2,3},{3,2},{4,5},{5,4},{6,7},{7,6},{8,9},{9,8},{10,11... | collective-permute-start | bytes 4718600 | tf_op jit(solution)/shard_map/ppermute | solution.py:1222
  314.9 71.5 %collective-permute-start.27 = (bf16[768,1536]{1,0:T(8,128)(2,1)}, bf16[768,1536]{1,0:T(8,128)(2,1)S(1)}, u32[]{:S(2)}, u32[]{:S(2)}) collective-permute-start(bf16[768,1536]{1,0:T(8,128)(2,1)} %get-tuple-element.120), channel_id=1, source_target_pairs={{0,1},{1,0},{2,3},{3,2},{4,5},{5,4},{6,7},{7,6},{8,9},{9,8},{10,11... | collective-permute-start | bytes 7077896 | tf_op jit(solution)/shard_map/ppermute | solution.py:1222
  315.5 17.9 %collective-permute-start.21 = (bf16[192,192]{1,0:T(8,128)(2,1)S(1)}, bf16[192,192]{1,0:T(8,128)(2,1)S(1)}, u32[]{:S(2)}, u32[]{:S(2)}) collective-permute-start(bf16[192,192]{1,0:T(8,128)(2,1)S(1)} %slice.376), channel_id=1, source_target_pairs={{0,4},{2,6},{4,0},{6,2},{1,5},{3,7},{5,1},{7,3},{8,12},{10,14},{12... | collective-permute-start | bytes 221192 | tf_op jit(solution)/shard_map/ppermute | solution.py:832
  317.5 17.3 %collective-permute-start.23 = (bf16[192,192]{1,0:T(8,128)(2,1)S(1)}, bf16[192,192]{1,0:T(8,128)(2,1)S(1)}, u32[]{:S(2)}, u32[]{:S(2)}) collective-permute-start(bf16[192,192]{1,0:T(8,128)(2,1)S(1)} %slice.382), channel_id=1, source_target_pairs={{0,2},{2,0},{4,6},{6,4},{1,3},{3,1},{5,7},{7,5},{8,10},{10,8},{12,... | collective-permute-start | bytes 221192 | tf_op jit(solution)/shard_map/ppermute | solution.py:833
  333.5 12.7 %collective-permute-start.12 = (bf16[384,576]{1,0:T(8,128)(2,1)S(1)}, bf16[384,576]{1,0:T(8,128)(2,1)S(1)}, u32[]{:S(2)}, u32[]{:S(2)}) collective-permute-start(bf16[384,576]{1,0:T(8,128)(2,1)S(1)} %slice.355), channel_id=1, source_target_pairs={{0,2},{2,0},{4,6},{6,4},{1,3},{3,1},{5,7},{7,5},{8,10},{10,8},{12,... | collective-permute-start | bytes 1327112 | tf_op jit(solution)/shard_map/ppermute | solution.py:828
  334.8 13.2 %collective-permute-start.14 = (bf16[384,576]{1,0:T(8,128)(2,1)S(1)}, bf16[384,576]{1,0:T(8,128)(2,1)S(1)}, u32[]{:S(2)}, u32[]{:S(2)}) collective-permute-start(bf16[384,576]{1,0:T(8,128)(2,1)S(1)} %pad_maximum_fusion.2), channel_id=1, source_target_pairs={{0,4},{2,6},{4,0},{6,2},{1,5},{3,7},{5,1},{7,3},{8,12},{10,14},{12... | collective-permute-start | bytes 1327112 | tf_op jit(solution)/shard_map/ppermute | solution.py:829
  346.2 16.9 %collective-permute-start.24 = (bf16[48,384]{1,0:T(8,128)(2,1)S(1)}, bf16[48,384]{1,0:T(8,128)(2,1)S(1)}, u32[]{:S(2)}, u32[]{:S(2)}) collective-permute-start(bf16[48,384]{1,0:T(8,128)(2,1)S(1)} %get-tuple-element.173), channel_id=1, source_target_pairs={{0,8},{8,0},{16,24},{24,16},{1,9},{9,1},{17,25},{25,17},{2,10},{10... | collective-permute-start | bytes 110600 | tf_op jit(solution)/shard_map/ppermute | solution.py:838
  362.9 26.5 %collective-permute-start.35 = (bf16[768,1536]{1,0:T(8,128)(2,1)S(1)}, bf16[768,1536]{1,0:T(8,128)(2,1)S(1)}, u32[]{:S(2)}, u32[]{:S(2)}) collective-permute-start(bf16[768,1536]{1,0:T(8,128)(2,1)S(1)} %copy-done.20), channel_id=1, source_target_pairs={{0,1},{1,0},{2,3},{3,2},{4,5},{5,4},{6,7},{7,6},{8,9},{9,8},{10,11... | collective-permute-start | bytes 7077896 | tf_op jit(solution)/shard_map/ppermute | solution.py:1222
  387.1 16.3 %collective-permute-start.28 = (bf16[384,768]{1,0:T(8,128)(2,1)S(1)}, bf16[384,768]{1,0:T(8,128)(2,1)S(1)}, u32[]{:S(2)}, u32[]{:S(2)}) collective-permute-start(bf16[384,768]{1,0:T(8,128)(2,1)S(1)} %slice.390), channel_id=1, source_target_pairs={{0,2},{2,0},{4,6},{6,4},{1,3},{3,1},{5,7},{7,5},{8,10},{10,8},{12,... | collective-permute-start | bytes 1769480 | tf_op jit(solution)/shard_map/ppermute | solution.py:828
  388.4 16.3 %collective-permute-start.30 = (bf16[384,768]{1,0:T(8,128)(2,1)S(1)}, bf16[384,768]{1,0:T(8,128)(2,1)S(1)}, u32[]{:S(2)}, u32[]{:S(2)}) collective-permute-start(bf16[384,768]{1,0:T(8,128)(2,1)S(1)} %pad_maximum_fusion), channel_id=1, source_target_pairs={{0,4},{2,6},{4,0},{6,2},{1,5},{3,7},{5,1},{7,3},{8,12},{10,14},{12... | collective-permute-start | bytes 1769480 | tf_op jit(solution)/shard_map/ppermute | solution.py:829
  390.1 26.0 %collective-permute-start.36 = (bf16[384,768]{1,0:T(8,128)(2,1)S(1)}, bf16[384,768]{1,0:T(8,128)(2,1)S(1)}, u32[]{:S(2)}, u32[]{:S(2)}) collective-permute-start(bf16[384,768]{1,0:T(8,128)(2,1)S(1)} %slice.406), channel_id=1, source_target_pairs={{0,2},{2,0},{4,6},{6,4},{1,3},{3,1},{5,7},{7,5},{8,10},{10,8},{12,... | collective-permute-start | bytes 1769480 | tf_op jit(solution)/shard_map/ppermute | solution.py:828
  391.3 26.1 %collective-permute-start.38 = (bf16[384,768]{1,0:T(8,128)(2,1)S(1)}, bf16[384,768]{1,0:T(8,128)(2,1)S(1)}, u32[]{:S(2)}, u32[]{:S(2)}) collective-permute-start(bf16[384,768]{1,0:T(8,128)(2,1)S(1)} %pad_maximum_fusion.1), channel_id=1, source_target_pairs={{0,4},{2,6},{4,0},{6,2},{1,5},{3,7},{5,1},{7,3},{8,12},{10,14},{12... | collective-permute-start | bytes 1769480 | tf_op jit(solution)/shard_map/ppermute | solution.py:829
  403.6 20.1 %collective-permute-start.29 = (bf16[192,768]{1,0:T(8,128)(2,1)S(1)}, bf16[192,768]{1,0:T(8,128)(2,1)S(1)}, u32[]{:S(2)}, u32[]{:S(2)}) collective-permute-start(bf16[192,768]{1,0:T(8,128)(2,1)S(1)} %slice.392), channel_id=1, source_target_pairs={{0,4},{2,6},{4,0},{6,2},{1,5},{3,7},{5,1},{7,3},{8,12},{10,14},{12... | collective-permute-start | bytes 884744 | tf_op jit(solution)/shard_map/ppermute | solution.py:832
  404.9 18.9 %collective-permute-start.31 = (bf16[192,768]{1,0:T(8,128)(2,1)S(1)}, bf16[192,768]{1,0:T(8,128)(2,1)S(1)}, u32[]{:S(2)}, u32[]{:S(2)}) collective-permute-start(bf16[192,768]{1,0:T(8,128)(2,1)S(1)} %slice.398), channel_id=1, source_target_pairs={{0,2},{2,0},{4,6},{6,4},{1,3},{3,1},{5,7},{7,5},{8,10},{10,8},{12,... | collective-permute-start | bytes 884744 | tf_op jit(solution)/shard_map/ppermute | solution.py:833
  416.2 11.2 %collective-permute-start.37 = (bf16[192,768]{1,0:T(8,128)(2,1)S(1)}, bf16[192,768]{1,0:T(8,128)(2,1)S(1)}, u32[]{:S(2)}, u32[]{:S(2)}) collective-permute-start(bf16[192,768]{1,0:T(8,128)(2,1)S(1)} %slice.408), channel_id=1, source_target_pairs={{0,4},{2,6},{4,0},{6,2},{1,5},{3,7},{5,1},{7,3},{8,12},{10,14},{12... | collective-permute-start | bytes 884744 | tf_op jit(solution)/shard_map/ppermute | solution.py:832
  417.6 10.0 %collective-permute-start.39 = (bf16[192,768]{1,0:T(8,128)(2,1)S(1)}, bf16[192,768]{1,0:T(8,128)(2,1)S(1)}, u32[]{:S(2)}, u32[]{:S(2)}) collective-permute-start(bf16[192,768]{1,0:T(8,128)(2,1)S(1)} %slice.414), channel_id=1, source_target_pairs={{0,2},{2,0},{4,6},{6,4},{1,3},{3,1},{5,7},{7,5},{8,10},{10,8},{12,... | collective-permute-start | bytes 884744 | tf_op jit(solution)/shard_map/ppermute | solution.py:833
  423.9 11.1 %collective-permute-start.32 = (bf16[48,1536]{1,0:T(8,128)(2,1)S(1)}, bf16[48,1536]{1,0:T(8,128)(2,1)S(1)}, u32[]{:S(2)}, u32[]{:S(2)}) collective-permute-start(bf16[48,1536]{1,0:T(8,128)(2,1)S(1)} %get-tuple-element.158), channel_id=1, source_target_pairs={{0,8},{8,0},{16,24},{24,16},{1,9},{9,1},{17,25},{25,17},{2,10},{10... | collective-permute-start | bytes 442376 | tf_op jit(solution)/shard_map/ppermute | solution.py:838
  424.0 11.3 %collective-permute-start.34 = (bf16[48,1536]{1,0:T(8,128)(2,1)S(1)}, bf16[48,1536]{1,0:T(8,128)(2,1)S(1)}, u32[]{:S(2)}, u32[]{:S(2)}) collective-permute-start(bf16[48,1536]{1,0:T(8,128)(2,1)S(1)} %get-tuple-element.159), channel_id=1, source_target_pairs={{0,24},{8,16},{16,8},{24,0},{1,25},{9,17},{17,9},{25,1},{2,26},{10... | collective-permute-start | bytes 442376 | tf_op jit(solution)/shard_map/ppermute | solution.py:838
  426.3 18.1 %collective-permute-start.33 = (bf16[48,1536]{1,0:T(8,128)(2,1)S(1)}, bf16[48,1536]{1,0:T(8,128)(2,1)S(1)}, u32[]{:S(2)}, u32[]{:S(2)}) collective-permute-start(bf16[48,1536]{1,0:T(8,128)(2,1)S(1)} %get-tuple-element.160), channel_id=1, source_target_pairs={{0,16},{8,24},{16,0},{24,8},{1,17},{9,25},{17,1},{25,9},{2,18},{10... | collective-permute-start | bytes 442376 | tf_op jit(solution)/shard_map/ppermute | solution.py:838
  427.7 17.6 %collective-permute-start.40 = (bf16[48,1536]{1,0:T(8,128)(2,1)S(1)}, bf16[48,1536]{1,0:T(8,128)(2,1)S(1)}, u32[]{:S(2)}, u32[]{:S(2)}) collective-permute-start(bf16[48,1536]{1,0:T(8,128)(2,1)S(1)} %get-tuple-element.155), channel_id=1, source_target_pairs={{0,8},{8,0},{16,24},{24,16},{1,9},{9,1},{17,25},{25,17},{2,10},{10... | collective-permute-start | bytes 442376 | tf_op jit(solution)/shard_map/ppermute | solution.py:838
  428.7 16.5 %collective-permute-start.42 = (bf16[48,1536]{1,0:T(8,128)(2,1)S(1)}, bf16[48,1536]{1,0:T(8,128)(2,1)S(1)}, u32[]{:S(2)}, u32[]{:S(2)}) collective-permute-start(bf16[48,1536]{1,0:T(8,128)(2,1)S(1)} %get-tuple-element.156), channel_id=1, source_target_pairs={{0,24},{8,16},{16,8},{24,0},{1,25},{9,17},{17,9},{25,1},{2,26},{10... | collective-permute-start | bytes 442376 | tf_op jit(solution)/shard_map/ppermute | solution.py:838
  435.0 12.6 %collective-permute-start.41 = (bf16[48,1536]{1,0:T(8,128)(2,1)S(1)}, bf16[48,1536]{1,0:T(8,128)(2,1)S(1)}, u32[]{:S(2)}, u32[]{:S(2)}) collective-permute-start(bf16[48,1536]{1,0:T(8,128)(2,1)S(1)} %get-tuple-element.157), channel_id=1, source_target_pairs={{0,16},{8,24},{16,0},{24,8},{1,17},{9,25},{17,1},{25,9},{2,18},{10... | collective-permute-start | bytes 442376 | tf_op jit(solution)/shard_map/ppermute | solution.py:838
  (36 other events, 155.5 us)
